TPU v7x, 32 devices: a whole 2x2x4 slice. The times are simulated.
32 devices in a mesh: row: 4 (over z), col: 8 (over y, x, core).
Axes of the slice: x: 2, y: 2, z: 4, core: 2. Of those that a mesh axis runs over, the one named last changes fastest.
Arguments:
- t2_pairs: bfloat16 [8, 8, 16, 16, 64, 64], P('row', None, None, None, 'col'), may hold values from -6 to 6
- cycle_ints: bfloat16 [8192, 8192], P('row', 'col'), may hold values from -0.1875 to 0.1875
- eps_occ: float32 [8, 16], replicated, may hold values from -2 to -0.4
- eps_virt: float32 [8, 64], replicated, may hold values from 0.2 to 3
- occ_count: int32 [8], replicated, may hold values from 8 to 16, as said below
- virt_count: int32 [8], replicated, may hold values from 32 to 64, as said below
- window_irrep: int32 [1], replicated, may hold values from 0 to 7
Outputs:
- update: float32 [8192, 8192], P('row', 'col')
Inputs may be any that keep to these rules, and one draw needn't show every extreme that they name: `occ_count`: at least half of the slots; one irrep fills all 16, and another holds exactly the least. `virt_count`: at least half of the slots; one irrep fills all 64, and another holds exactly the least.
All inputs are finite; a program needn't handle non-finite values.
Results may differ from a plain program's by a relative error of at most 0.0003.
Values may be sent and summed in bfloat16 or wider, within the bound.
No kernel may reach another device: no remote copies, remote signals or barrier semaphores. Data moves between devices by JAX's collectives and lax.ppermute only.
A program may use at most 128 MiB of HBM per device.

v0:
```python
import functools

import jax
import jax.numpy as jnp
from jax import lax
from jax.experimental import pallas as pl
from jax.experimental.pallas import tpu as pltpu
from jax.sharding import PartitionSpec as P

NIRREP = 8
OCC_CAP = 16
VIR_CAP = 64
BLOCK = VIR_CAP * OCC_CAP
SIZES = (1024, 896, 768, 640)
WIDE = 512
F32 = jnp.float32
BF16 = jnp.bfloat16
I32 = jnp.int32
I16 = jnp.int16
VMEM_BYTES = 56 * 1024 * 1024


def iota(shape, dim):
    return lax.broadcasted_iota(I32, shape, dim)


def params():
    return pltpu.CompilerParams(vmem_limit_bytes=VMEM_BYTES)


def cost(flops, nbytes):
    return pl.CostEstimate(flops=flops, bytes_accessed=nbytes, transcendentals=0)


def pair_scalars(occ, virt, win, pair):
    first = 2 * pair
    o_a, o_b = occ[first], occ[first + 1]
    v_a, v_b = virt[first ^ win[0]], virt[(first + 1) ^ win[0]]
    return (o_a, o_b), (v_a, v_b), (o_a * ((v_a + 1) >> 1), o_a * (v_a >> 1))


def place(q, p, second, counts):
    (o_a, o_b), (v_a, v_b), (start_even, start_odd) = counts
    o = jnp.where(second, o_b, o_a)
    v = jnp.where(second, v_b, v_a)
    start = jnp.where(second, jnp.where((q & 1) == 0, start_even, start_odd), 0)
    return jnp.where((p < o) & (q < v), start + (q >> 1) * o + p, -1)


def one_hot(left, right):
    return jnp.where(left.astype(I16) == right.astype(I16), BF16(1.0), BF16(0.0))


def dot(a, b):
    return jnp.dot(a, b, preferred_element_type=F32)


def prep_kernel(size, occ, virt, win, t2_ref, even_ref, odd_ref, x_ref):
    counts = pair_scalars(occ, virt, win, pl.program_id(0))
    row = iota((256, 1), 0)
    source = (((row >> 6) & 1) << 7) | (((row >> 2) & 15) << 3) | ((row & 3) << 1) | (row >> 7)
    by_parity = one_hot(iota((256, 256), 1), source)
    targets = []
    for half in range(2):
        for group in range(4):
            parts = [
                t2_ref[:, half, :, 4 * group + i].astype(F32).reshape(256, VIR_CAP) for i in range(4)
            ]
            x = jnp.concatenate(parts, axis=1).astype(BF16)
            at = (4 * half + group) * 256
            x_ref[:, at : at + 256] = dot(by_parity, x).astype(BF16)
            r = iota((256, 1), 0)
            p, q = 4 * group + (r >> 6), r & 63
            spot = place(q, p, half == 1, counts)
            targets.append(jnp.where(spot >= 0, spot + (q & 1) * size, -1))
    @pl.loop(0, 2)
    def _(core):
        for tile in range(-(-size // 256)):
            col = min(256 * tile, size - 256)
            lane = iota((256, 256), 1) + (col + core * size)
            acc = jnp.zeros((256, 256), F32)
            for chunk in range(4 if col >= BLOCK // 2 else 0, 8):
                acc += dot(x_ref[:, chunk * 256 : chunk * 256 + 256], one_hot(targets[chunk], lane))
            acc = acc.astype(BF16)
            even_ref[core, :, col : col + 256] = acc[:128]
            odd_ref[core, :, col : col + 256] = acc[128:]


def prep(size, scalars, t2):
    shape = jax.ShapeDtypeStruct((NIRREP, 128, size), BF16)
    block = pl.BlockSpec((2, 128, size), lambda k, *_: (k, 0, 0))
    return pl.pallas_call(
        functools.partial(prep_kernel, size),
        out_shape=(shape, shape),
        grid_spec=pltpu.PrefetchScalarGridSpec(
            num_scalar_prefetch=3,
            grid=(NIRREP // 2,),
            in_specs=[
                pl.BlockSpec((2, 2, OCC_CAP, OCC_CAP, 8, VIR_CAP), lambda k, *_: (0, k, 0, 0, 0, 0))
            ],
            out_specs=[block, block],
            scratch_shapes=[pltpu.VMEM((256, 2048), BF16)],
        ),
        compiler_params=params(),
        cost_estimate=cost(2 * 4 * 256 * 2048 * 2 * size, 12 * 2**20),
        name="prep_amplitudes",
    )(*scalars, t2)


def fill_rows(rows, spot, sel_ref):
    @pl.loop(0, rows // 128)
    def _(n):
        first = pl.multiple_of(n * 128, 128)
        sel_ref[pl.ds(first, 128), :] = one_hot(iota((128, BLOCK), 0) + first, spot)


def rows_kernel(rows, parity, count, occ, virt, win, at, x_ref, *refs):
    out_ref, sel_ref = refs[count], refs[-1]
    counts = pair_scalars(occ, virt, win, at[0])
    i = iota((1, BLOCK), 1)
    q = 8 * (i >> 7) + 2 * (i & 3) + parity
    spot = place(q, (i >> 2) & 15, ((i >> 6) & 1) == 1, counts)
    fill_rows(rows, spot, sel_ref)
    cols = out_ref.shape[1]

    @pl.loop(0, -(-cols // 256))
    def _(n):
        lanes = pl.ds(pl.multiple_of(jnp.minimum(n * 256, cols - 256), 128), 256)
        x = x_ref[:, :, lanes].reshape(BLOCK, 256)

        @pl.loop(0, 2)
        def _(half):
            at_rows = pl.ds(pl.multiple_of(half * (rows // 2), 64), rows // 2)
            out_ref[at_rows, lanes] = dot(sel_ref[at_rows, :], x).astype(BF16)


def compact_rows(rows, cols, parity, scalars, at, x, passed=(), awaited=()):
    whole = pl.BlockSpec(memory_space=pl.ANY)
    return pl.pallas_call(
        functools.partial(rows_kernel, rows, parity, len(passed) + len(awaited)),
        out_shape=[jax.ShapeDtypeStruct((rows, cols), BF16)]
        + [jax.ShapeDtypeStruct(y.shape, y.dtype) for y in passed],
        grid_spec=pltpu.PrefetchScalarGridSpec(
            num_scalar_prefetch=4,
            grid=(1,),
            in_specs=[pl.BlockSpec((NIRREP, 128, cols), lambda n, *_: (0, 0, 0))]
            + [whole] * (len(passed) + len(awaited)),
            out_specs=[pl.BlockSpec((rows, cols), lambda n, *_: (0, 0))] + [whole] * len(passed),
            scratch_shapes=[pltpu.VMEM((rows, BLOCK), BF16)],
        ),
        input_output_aliases={5 + i: 1 + i for i in range(len(passed))},
        compiler_params=params(),
        cost_estimate=cost(4 * rows * BLOCK * cols, 4 * rows * BLOCK),
        name="compact_rows",
    )(*scalars, at, x, *passed, *awaited)


def ints_kernel(rows, cols, occ, virt, win, at, mine_ref, other_ref, awaited, out_ref, sel_ref, cols_ref):
    plane, dev = at[0], at[1]
    parity = dev & 1

    @pl.when(pl.program_id(0) == 0)
    def _():
        counts = pair_scalars(occ, virt, win, plane)
        i = iota((1, BLOCK), 1)
        q = 2 * ((i >> 4) & 31) + parity
        spot = place(q, i & 15, (i >> 9) == 1, counts)
        fill_rows(rows, spot, sel_ref)

    counts = pair_scalars(occ, virt, win, dev >> 1)
    i = iota((BLOCK, 1), 0)
    q, p = i >> 4, i & 15
    lane = iota((BLOCK, 256), 1) + pl.program_id(0) * 256
    picks = []
    for second in (parity == 1, parity == 0):
        spot = place(q, p, second, counts)
        picks.append(one_hot(jnp.where(spot >= 0, spot + (q & 1) * cols, -1), lane))

    @pl.loop(0, 2)
    def _(half):
        at_rows = pl.ds(pl.multiple_of(half * (BLOCK // 2), BLOCK // 2), BLOCK // 2)
        acc = dot(mine_ref[half].reshape(BLOCK // 2, BLOCK), picks[0])
        acc += dot(other_ref[at_rows, :], picks[1])
        cols_ref[at_rows, :] = acc.astype(BF16)

    out_ref[...] = dot(sel_ref[...], cols_ref[...]).astype(BF16)


def compact_ints(rows, cols, scalars, at, mine, other, awaited):
    mine_spec = pl.BlockSpec(
        (2, VIR_CAP // 2, 1, OCC_CAP, BLOCK), lambda n, o, v, w, a: (0, 0, a[1] & 1, 0, 0)
    )
    whole = pl.BlockSpec((BLOCK, BLOCK), lambda n, *_: (0, 0))
    return pl.pallas_call(
        functools.partial(ints_kernel, rows, cols),
        out_shape=jax.ShapeDtypeStruct((rows, 2 * cols), BF16),
        grid_spec=pltpu.PrefetchScalarGridSpec(
            num_scalar_prefetch=4,
            grid=(2 * cols // 256,),
            in_specs=[mine_spec, whole, pl.BlockSpec(memory_space=pl.ANY)],
            out_specs=pl.BlockSpec((rows, 256), lambda n, *_: (0, n)),
            scratch_shapes=[pltpu.VMEM((rows, BLOCK), BF16), pltpu.VMEM((BLOCK, 256), BF16)],
        ),
        compiler_params=params(),
        cost_estimate=cost(16 * BLOCK * BLOCK * cols, 4 * BLOCK * BLOCK + 4 * rows * cols),
        name="compact_ints",
    )(*scalars, at, mine, other, awaited)


def widen_tile(rows, cols, tile, occ, virt, win, dev, own_refs, sib_refs, wide_ref):
    parity = dev & 1
    counts = pair_scalars(occ, virt, win, dev >> 1)
    (o_a, o_b), _, (start_even, start_odd) = counts
    second = parity == 1
    o = jnp.where(second, o_b, o_a)
    i = iota((1, 256), 1) + tile * 256
    q = i >> 4
    spot = place(q, i & 15, second, counts)
    r = iota((256, 256), 0)
    picks = []
    for s in (parity, 1 - parity):
        start = jnp.where(second, jnp.where(s == 0, start_even, start_odd), 0) + 8 * tile * o
        start = jnp.minimum((start >> 7) << 7, cols - 256)
        window = pl.ds(pl.multiple_of(start, 128), 256)
        picks.append((window, one_hot(r + start, jnp.where((q & 1) == s, spot, -1))))
    for piece in range(2):
        x = dot(own_refs[piece][:, picks[0][0]], picks[0][1])
        x += dot(sib_refs[piece][:, picks[1][0]], picks[1][1])
        wide_ref[piece * cols : piece * cols + rows, :] = x.astype(BF16)
        if rows < cols:
            wide_ref[piece * cols + rows : (piece + 1) * cols, :] = jnp.zeros((cols - rows, 256), BF16)


def widen_kernel(rows, cols, slots, occ, virt, win, at, *refs):
    wide_ref = refs[-1]
    for slot in range(slots):

        @pl.when(pl.program_id(0) == slot)
        def _():
            t0, t1, s0, s1 = refs[4 * slot : 4 * slot + 4]
            tile = pl.program_id(1)
            widen_tile(rows, cols, tile, occ, virt, win, at[1], (t0, t1), (s0, s1), wide_ref.at[0])


def widen(rows, cols, scalars, at, blocks):
    slots = len(blocks) // 4
    square = pl.BlockSpec((rows, cols), lambda t, n, *_: (0, 0), pipeline_mode=pl.Buffered(1))
    return pl.pallas_call(
        functools.partial(widen_kernel, rows, cols, slots),
        out_shape=jax.ShapeDtypeStruct((slots, 2 * cols, BLOCK), BF16),
        grid_spec=pltpu.PrefetchScalarGridSpec(
            num_scalar_prefetch=4,
            grid=(slots, BLOCK // 256),
            in_specs=[square] * len(blocks),
            out_specs=pl.BlockSpec((1, 2 * cols, 256), lambda t, n, *_: (t, 0, n)),
        ),
        compiler_params=params(),
        cost_estimate=cost(slots * 8 * rows * 512 * BLOCK, slots * (8 * rows * cols + 4 * cols * BLOCK)),
        name="widen",
    )(*scalars, at, *blocks)


def product_kernel(inner, ints_ref, wide_ref, acc_ref):
    at = pl.ds(pl.multiple_of(pl.program_id(1) * WIDE, WIDE), WIDE)

    @pl.when(pl.program_id(0) == 0)
    def _():
        acc_ref[:, :, at] = jnp.zeros((2, acc_ref.shape[1], WIDE), F32)

    @pl.loop(0, 2)
    def _(half):
        acc_ref[half, :, at] += dot(ints_ref[0, half], wide_ref[0])


def product(rows, cols, inner, ints, wide):
    slots = wide.shape[0]
    return pl.pallas_call(
        product_kernel,
        out_shape=jax.ShapeDtypeStruct((2, rows, BLOCK), F32),
        grid_spec=pltpu.PrefetchScalarGridSpec(
            num_scalar_prefetch=1,
            grid=(slots, BLOCK // WIDE),
            in_specs=[
                pl.BlockSpec((1, 2, rows, 2 * cols), lambda t, n, k: (k[t], 0, 0, 0)),
                pl.BlockSpec((1, 2 * cols, WIDE), lambda t, n, k: (t, 0, n)),
            ],
            out_specs=pl.BlockSpec((2, rows, BLOCK), lambda t, n, k: (0, 0, 0)),
        ),
        compiler_params=params(),
        cost_estimate=cost(16 * slots * rows * cols * BLOCK, slots * 4 * cols * (rows + BLOCK)),
        name="product",
    )(inner, ints, wide)


def last_kernel(
    rows, cols, occ, virt, win, at, inner,
    ints_ref, t0, t1, s0, s1, old_ref, evirt, eocc_ref, ecol_ref, out_ref, wide_ref, sum_ref,
):
    plane, dev = at[0], at[1]

    @pl.loop(0, WIDE // 256)
    def _(part):
        tile = pl.program_id(0) * (WIDE // 256) + part
        into = wide_ref.at[:, pl.ds(pl.multiple_of(part * 256, 256), 256)]
        widen_tile(rows, cols, tile, occ, virt, win, dev, (t0, t1), (s0, s1), into)

    @pl.loop(0, 2)
    def _(half):
        sum_ref[half, :rows, :] = old_ref[half] + dot(ints_ref[0, half], wide_ref[...])

    i = iota((1, WIDE), 1) + pl.program_id(0) * WIDE
    col_live = ((i & 15) < occ[dev]) & ((i >> 4) < virt[dev ^ win[0]])
    col_energy = ecol_ref[...]
    _, _, starts = pair_scalars(occ, virt, win, plane)
    p = iota((OCC_CAP, 1), 0)
    irreps = [2 * plane, 2 * plane + 1]
    occs = [occ[irrep] for irrep in irreps]
    partners = [irrep ^ win[0] for irrep in irreps]
    virts = [virt[partner] for partner in partners]
    live = [(p < o) & col_live for o in occs]

    @pl.loop(0, VIR_CAP // 4)
    def _(group):
        for h in range(2):
            for i in range(4):
                half_q, s = 2 * group + i // 2, i % 2
                q = 2 * half_q + s
                start = half_q * occs[h]
                if h == 1:
                    start = start + starts[s]
                start = jnp.minimum(start, rows)
                block = sum_ref[s, pl.ds(pl.multiple_of((start >> 3) << 3, 8), OCC_CAP + 8), :]
                block = pltpu.roll(block, OCC_CAP + 8 - (start & 7), 0)[:OCC_CAP]
                denom = (eocc_ref[h] - evirt[partners[h], q]) + col_energy
                value = jnp.where(live[h] & (q < virts[h]), block / denom, 0.0)
                at_row = pl.multiple_of((h * VIR_CAP + q) * OCC_CAP, OCC_CAP)
                out_ref[pl.ds(at_row, OCC_CAP), :] = value


def last(rows, cols, scalars, at, inner, ints, own, sib, acc, energies):
    square = pl.BlockSpec((rows, cols), lambda n, *_: (0, 0))
    return pl.pallas_call(
        functools.partial(last_kernel, rows, cols),
        out_shape=jax.ShapeDtypeStruct((2 * BLOCK, BLOCK), F32),
        grid_spec=pltpu.PrefetchScalarGridSpec(
            num_scalar_prefetch=5,
            grid=(BLOCK // WIDE,),
            in_specs=[
                pl.BlockSpec((1, 2, rows, 2 * cols), lambda n, o, v, w, a, k: (k[0], 0, 0, 0)),
                square, square, square, square,
                pl.BlockSpec((2, rows, WIDE), lambda n, *_: (0, 0, n)),
                pl.BlockSpec(memory_space=pltpu.SMEM),
                pl.BlockSpec((2, OCC_CAP, 1), lambda n, *_: (0, 0, 0)),
                pl.BlockSpec((1, WIDE), lambda n, *_: (0, n)),
            ],
            out_specs=pl.BlockSpec((2 * BLOCK, WIDE), lambda n, *_: (0, n)),
            scratch_shapes=[
                pltpu.VMEM((2 * cols, WIDE), BF16),
                pltpu.VMEM((2, rows + OCC_CAP + 8, WIDE), F32),
            ],
        ),
        compiler_params=params(),
        cost_estimate=cost(16 * rows * cols * BLOCK, 8 * rows * cols + 16 * rows * BLOCK),
        name="last_product",
    )(*scalars, at, inner, ints, *own, *sib, acc, *energies)


def after_kernel(*refs):
    pass


def after(kept, awaited):
    whole = pl.BlockSpec(memory_space=pl.ANY)
    return pl.pallas_call(
        after_kernel,
        out_shape=[jax.ShapeDtypeStruct(x.shape, x.dtype) for x in kept],
        in_specs=[whole] * (len(kept) + len(awaited)),
        out_specs=[whole] * len(kept),
        input_output_aliases={i: i for i in range(len(kept))},
        name="after",
    )(*kept, *awaited)


def ring_order(n):
    return list(range(0, 1)) + list(range(1, n, 2)) + [i for i in range(n - 1, 0, -1) if i % 2 == 0]


def branch(rows, nrow, ncol, t2, ints, occ, virt, win, eps_virt, occ_rows, col_energy, at, sources):
    cols = -(-rows // 128) * 128
    scalars = (occ, virt, win)
    order = ring_order(nrow)
    ring = [(order[i], order[(i + 1) % nrow]) for i in range(nrow)]
    swap = [(c, c ^ 1) for c in range(ncol)]

    def to_sibling(x):
        return lax.ppermute(x, "col", swap)

    def around(x):
        return lax.ppermute(x, "row", ring)

    def exchange(x):
        return lax.all_to_all(x, "col", split_axis=0, concat_axis=0, tiled=True)

    even, odd = prep(cols, scalars, t2)
    even, odd = compact_rows(rows, cols, 0, scalars, at, exchange(even), passed=(odd,))
    mine = ints.reshape(2, VIR_CAP // 2, 2, OCC_CAP, BLOCK)
    other = lax.dynamic_index_in_dim(mine, 1 - (at[1] & 1), 2, keepdims=False).reshape(BLOCK, BLOCK)
    even_next = around(even)
    small = compact_ints(rows, cols, scalars, at, mine, to_sibling(other), even)
    odd, small = compact_rows(rows, cols, 1, scalars, at, exchange(odd), passed=(small,))
    odd, small = after([odd, small], [even_next])
    panel = lax.all_gather(small, "col", axis=0, tiled=False).reshape(ncol // 2, 2, rows, 2 * cols)

    held = [even, odd]
    blocks = []
    for step in range(nrow - 1):
        later = [even_next if step == 0 else around(held[0]), around(held[1])]
        blocks += held + [to_sibling(x) for x in held]
        held = later
    wide = widen(rows, cols, scalars, at, blocks)
    acc = product(rows, cols, sources[: nrow - 1], panel, wide)
    own = after(held, [acc])
    sib = [to_sibling(x) for x in own]
    energies = (eps_virt, occ_rows, col_energy)
    return last(rows, cols, scalars, at, sources[nrow - 1 :], panel, own, sib, acc, energies)


def choose_kernel(occ, virt, win, index_ref):
    index = jnp.int32(len(SIZES) - 1)
    for pair in range(NIRREP // 2):
        (o_a, o_b), (v_a, v_b), _ = pair_scalars(occ, virt, win, pair)
        most = o_a * ((v_a + 1) >> 1) + o_b * ((v_b + 1) >> 1)
        fits = sum((most <= size).astype(I32) for size in SIZES[1:])
        index = jnp.minimum(index, fits)
    index_ref[0] = index


def choose(occ, virt, win):
    smem = pl.BlockSpec(memory_space=pltpu.SMEM)
    return pl.pallas_call(
        choose_kernel,
        out_shape=jax.ShapeDtypeStruct((1,), I32),
        in_specs=[smem] * 3,
        out_specs=smem,
        name="choose",
    )(occ, virt, win)[0]


def live_device(nrow, ncol, t2, ints, eps_occ, eps_virt, occ, virt, win):
    row, col = lax.axis_index("row"), lax.axis_index("col")
    index = choose(occ, virt, win)
    occ_rows = lax.dynamic_slice(eps_occ, (2 * row, 0), (2, OCC_CAP)).reshape(2, OCC_CAP, 1)
    col_occ = lax.dynamic_slice(eps_occ, (col, 0), (1, OCC_CAP))
    col_virt = lax.dynamic_slice(eps_virt, (col ^ win[0], 0), (1, VIR_CAP))
    col_energy = (col_occ[:, None, :] - col_virt[:, :, None]).reshape(1, BLOCK)
    at = jnp.stack([row, col]).astype(I32)
    order = ring_order(nrow)
    table = [[order[(order.index(z) - t) % nrow] for t in range(nrow)] for z in range(nrow)]
    sources = lax.dynamic_slice(jnp.array(table, I32), (row, 0), (1, nrow)).reshape(nrow)
    operands = (t2, ints, occ, virt, win, eps_virt, occ_rows, col_energy, at, sources)
    return lax.switch(index, [functools.partial(branch, size, nrow, ncol) for size in SIZES], *operands)


def ph_vectors(eps_occ, eps_virt, occ_count, virt_count, window_irrep):
    irreps = jnp.arange(NIRREP, dtype=I32)
    partner = jnp.bitwise_xor(irreps, window_irrep[0])
    onehot = partner[:, None] == irreps[None, :]
    virt_rows = jnp.dot(onehot.astype(F32), eps_virt, precision=lax.Precision.HIGHEST)
    virt_live = jnp.sum(jnp.where(onehot, virt_count[None, :], 0), axis=1)
    energy = eps_occ[:, None, :] - virt_rows[:, :, None]
    slots_occ = jnp.arange(OCC_CAP, dtype=I32)
    slots_virt = jnp.arange(VIR_CAP, dtype=I32)
    live = (slots_occ[None, None, :] < occ_count[:, None, None]) & (
        slots_virt[None, :, None] < virt_live[:, None, None]
    )
    return (energy, live)


def any_device(t2_pairs, cycle_ints, eps_occ, eps_virt, occ_count, virt_count, window_irrep):
    irrep_local = t2_pairs.shape[0]
    virt_local = t2_pairs.shape[4]
    total = NIRREP * VIR_CAP * OCC_CAP
    energy, live = ph_vectors(eps_occ, eps_virt, occ_count, virt_count, window_irrep)
    row_index = lax.axis_index("row")
    col_index = lax.axis_index("col")
    zero_index = jnp.int32(0)
    source_live = lax.dynamic_slice(
        live,
        (row_index * irrep_local, col_index * virt_local, zero_index),
        (irrep_local, virt_local, OCC_CAP),
    )
    full_live = live.reshape(-1)
    ordered = jnp.transpose(t2_pairs, (0, 4, 2, 1, 5, 3)).reshape(
        irrep_local, virt_local, OCC_CAP, total
    )
    keep = source_live[:, :, :, None] & full_live[None, None, None, :]
    ordered = jnp.where(keep, ordered, jnp.zeros_like(ordered))
    moved = lax.all_to_all(ordered, "col", split_axis=3, concat_axis=1, tiled=True)
    amp_local = moved.reshape(irrep_local * VIR_CAP * OCC_CAP, moved.shape[3])
    amp_panel = lax.all_gather(amp_local, "row", axis=0, tiled=True)
    ints_panel = lax.all_gather(cycle_ints, "col", axis=1, tiled=True)
    cycle = jnp.dot(ints_panel, amp_panel, preferred_element_type=F32)
    rows_here, cols_here = cycle.shape
    flat_energy = energy.reshape(-1)
    row_start, col_start = row_index * rows_here, col_index * cols_here
    row_energy = lax.dynamic_slice_in_dim(flat_energy, row_start, rows_here, 0)
    col_energy = lax.dynamic_slice_in_dim(flat_energy, col_start, cols_here, 0)
    row_live = lax.dynamic_slice_in_dim(full_live, row_start, rows_here, 0)
    col_live = lax.dynamic_slice_in_dim(full_live, col_start, cols_here, 0)
    denom = row_energy[:, None] + col_energy[None, :]
    return jnp.where(row_live[:, None] & col_live[None, :], cycle / denom, F32(0.0))


def solution(mesh):
    nrow, ncol = mesh.shape["row"], mesh.shape["col"]
    placed = (P("row", None, None, None, "col", None), P("row", "col"), P(), P(), P(), P(), P())
    body = any_device
    if 2 * nrow == NIRREP and ncol == NIRREP:
        body = functools.partial(live_device, nrow, ncol)
    return jax.shard_map(body, mesh=mesh, in_specs=placed, out_specs=P("row", "col"), check_vma=False)
```

profile of v0, /device:TPU:0, one launch (start us, length us, event | category | flops | bytes accessed | tf_op | source)
XLA Modules:
  0.0 215.9 jit_solution(12204467406475537635)
XLA Ops:
  7.3 1.2 choose.1
  9.1 199.9 %conditional.1 = (f32[2048,1024]{1,0:T(8,128)}) conditional(s32[]{:T(128)} %bitcast.36, ((), s32[8]{0:T(128)}, s32[8]{0:T(128)}, s32[1]{0:T(128)}, bf16[2,8,16,16,8,64]{5,4,3,2,1,0:T(8,128)(2,1)}, /*index=5*/s32[2]{0:T(128)S(1)}, bf16[2048,1024]{1,0:T(8,128)(2,1)}, s32[]{:T(128)}, f32[8,64]{1,0:T(8,128)}, ...), branch_computations={%region_0.1_spmd, %region_1.2_spmd, %region_2.3_spmd, %region_3.4_... | conditional | flops 115964116992 | bytes 415283904 | solution.py:461
  9.4 1.8 constant_dynamic-slice_fusion.19
  11.7 15.7 %prep_amplitudes.7 = (bf16[8,128,640]{2,1,0:T(8,128)(2,1)}, bf16[8,128,640]{2,1,0:T(8,128)(2,1)}) custom-call(s32[8]{0:T(128)S(1)} %copy-done.26, s32[8]{0:T(128)S(1)} %copy-done.30, s32[1]{0:T(128)} %get-tuple-element.163.win, bf16[2,8,16,16,8,64]{5,4,3,2,1,0:T(8,128)(2,1)} %get-tuple-element.222.t2_ref), custom_call_target="tpu_custom_call" | custom-call | flops 5368709120 | bytes 12582912 | tf_op jit(solution)/shard_map/cond/branch_3_fun/prep_amplitudes/pallas_call | solution.py:92
  27.5 23.6 %all_to_all.33.x_ref = bf16[8,128,640]{2,1,0:T(8,128)(2,1)} all-to-all(bf16[8,128,640]{2,1,0:T(8,128)(2,1)} %get-tuple-element.167), channel_id=1, replica_groups=mesh['row'=4,'col'=8] {'col'}, dimensions={0} | all-to-all | bytes 2621440 | tf_op jit(solution)/shard_map/cond/branch_3_fun/all_to_all | solution.py:402
  51.0 5.8 %compact_rows.14 = (bf16[640,640]{1,0:T(8,128)(2,1)}, bf16[8,128,640]{2,1,0:T(8,128)(2,1)}) custom-call(s32[8]{0:T(128)S(1)} %copy-done.26, s32[8]{0:T(128)S(1)} %copy-done.30, s32[1]{0:T(128)} %get-tuple-element.163.win, s32[2]{0:T(128)S(1)} %get-tuple-element.164.at, bf16[8,128,640]{2,1,0:T(8,128)(2,1)} %all_to_all.33.x_ref, ...), custom_call_target="tpu_custom_call", output_to_operand_aliasing={{1}: (5, {})} | custom-call | flops 1677721600 | bytes 2621440 | tf_op jit(solution)/shard_map/cond/branch_3_fun/compact_rows/pallas_call | solution.py:139
  56.8 3.6 %all-to-all-start.7 = ((bf16[8,128,640]{2,1,0:T(8,128)(2,1)}), bf16[8,128,640]{2,1,0:T(8,128)(2,1)S(1)}, u32[]{:S(2)}, u32[]{:S(2)}) async-start(bf16[8,128,640]{2,1,0:T(8,128)(2,1)} %get-tuple-element.169), calls=%async_computation.7 | async-start | bytes 2621440 | tf_op jit(solution)/shard_map/cond/branch_3_fun/all_to_all | solution.py:402
  60.4 1.6 collective-permute-start.46
  62.0 18.5 %compact_ints.7.refs_0_ = bf16[640,1280]{1,0:T(8,128)(2,1)} custom-call(s32[8]{0:T(128)S(1)} %copy-done.26, s32[8]{0:T(128)S(1)} %copy-done.30, s32[1]{0:T(128)} %get-tuple-element.163.win, s32[2]{0:T(128)S(1)} %get-tuple-element.164.at, bf16[2,32,2,16,1024]{4,3,2,1,0:T(8,128)(2,1)} %bitcast.72, bf16[1024,1024]{1,0:T(8,128)(2,1)} %collective-permute-done.45.other_ref, ...), custom_call_target="tpu_custom_call" | custom-call | flops 10737418240 | bytes 5832704 | tf_op jit(solution)/shard_map/cond/branch_3_fun/compact_ints/pallas_call | solution.py:194
  80.6 1.1 copy-done.11
  81.6 5.8 %compact_rows.15 = (bf16[640,640]{1,0:T(8,128)(2,1)}, bf16[640,1280]{1,0:T(8,128)(2,1)}) custom-call(s32[8]{0:T(128)S(1)} %copy-done.26, s32[8]{0:T(128)S(1)} %copy-done.30, s32[1]{0:T(128)} %get-tuple-element.163.win, s32[2]{0:T(128)S(1)} %get-tuple-element.164.at, bf16[8,128,640]{2,1,0:T(8,128)(2,1)} %copy-done.11, ...), custom_call_target="tpu_custom_call", output_to_operand_aliasing={{1}: (5, {})} | custom-call | flops 1677721600 | bytes 2621440 | tf_op jit(solution)/shard_map/cond/branch_3_fun/compact_rows/pallas_call | solution.py:139
  87.4 2.7 %collective-permute-start.49 = (bf16[640,640]{1,0:T(8,128)(2,1)}, bf16[640,640]{1,0:T(8,128)(2,1)}, u32[]{:S(2)}, u32[]{:S(2)}) collective-permute-start(bf16[640,640]{1,0:T(8,128)(2,1)} %get-tuple-element.176.refs_1_), channel_id=1, source_target_pairs={{0,8},{8,24},{24,16},{16,0},{1,9},{9,25},{25,17},{17,1},{2,10},{10... | collective-permute-start | bytes 2457608 | tf_op jit(solution)/shard_map/cond/branch_3_fun/ppermute | solution.py:399
  90.5 19.3 %collective-permute-done.49.refs_5_ = bf16[640,640]{1,0:T(8,128)(2,1)} collective-permute-done((bf16[640,640]{1,0:T(8,128)(2,1)}, bf16[640,640]{1,0:T(8,128)(2,1)}, u32[]{:S(2)}, u32[]{:S(2)}) %collective-permute-start.49) | collective-permute-done | bytes 819232 | tf_op jit(solution)/shard_map/cond/branch_3_fun/ppermute | solution.py:399
  109.8 1.7 collective-permute-start.50
  112.0 15.2 %collective-permute-done.47.refs_8_ = bf16[640,640]{1,0:T(8,128)(2,1)S(1)} collective-permute-done((bf16[640,640]{1,0:T(8,128)(2,1)}, bf16[640,640]{1,0:T(8,128)(2,1)S(1)}, u32[]{:S(2)}, u32[]{:S(2)}) %collective-permute-start.47) | collective-permute-done | bytes 819232 | tf_op jit(solution)/shard_map/cond/branch_3_fun/ppermute | solution.py:399
  127.3 0.9 copy-done.40
  128.6 15.3 %collective-permute-done.50.refs_9_ = bf16[640,640]{1,0:T(8,128)(2,1)} collective-permute-done((bf16[640,640]{1,0:T(8,128)(2,1)}, bf16[640,640]{1,0:T(8,128)(2,1)}, u32[]{:S(2)}, u32[]{:S(2)}) %collective-permute-start.50) | collective-permute-done | bytes 819232 | tf_op jit(solution)/shard_map/cond/branch_3_fun/ppermute | solution.py:399
  144.0 0.7 constant_dynamic-slice_fusion.18
  145.2 1.7 collective-permute-start.48
  146.9 1.4 collective-permute-start.51
  148.3 0.9 copy-done.41
  149.2 14.0 %widen.7.wide_ref = bf16[3,1280,1024]{2,1,0:T(8,128)(2,1)} custom-call(s32[8]{0:T(128)S(1)} %copy-done.26, s32[8]{0:T(128)S(1)} %copy-done.30, s32[1]{0:T(128)} %get-tuple-element.163.win, s32[2]{0:T(128)S(1)} %get-tuple-element.164.at, bf16[640,640]{1,0:T(8,128)(2,1)} %get-tuple-element.172.awaited.refs_0_, bf16[640,640]{1,0:T(8,128)(2,1)} %get-tuple-element.176.refs_1_, ...), custom_call_target="tpu_custom_call" | custom-call | flops 8053063680 | bytes 17694720 | tf_op jit(solution)/shard_map/cond/branch_3_fun/widen/pallas_call | solution.py:248
  163.2 18.2 %product.7.refs_2_.old_ref = f32[2,640,1024]{2,1,0:T(8,128)} custom-call(s32[3]{0:T(128)} %slice_bitcast_fusion.3.inner, bf16[4,2,640,1280]{3,2,1,0:T(8,128)(2,1)} %bitcast.73, bf16[3,1280,1024]{2,1,0:T(8,128)(2,1)} %widen.7.wide_ref), custom_call_target="tpu_custom_call" | custom-call | flops 20132659200 | bytes 12779520 | tf_op jit(solution)/shard_map/cond/branch_3_fun/product/pallas_call | solution.py:277
  181.4 2.9 %collective-permute-done.51.refs_1_ = bf16[640,640]{1,0:T(8,128)(2,1)S(1)} collective-permute-done((bf16[640,640]{1,0:T(8,128)(2,1)}, bf16[640,640]{1,0:T(8,128)(2,1)S(1)}, u32[]{:S(2)}, u32[]{:S(2)}) %collective-permute-start.51) | collective-permute-done | bytes 819232 | tf_op jit(solution)/shard_map/cond/branch_3_fun/ppermute | solution.py:399
  184.3 0.9 copy-done.3
  186.4 0.6 slice.30
  187.1 0.7 fusion.10
  187.9 0.7 fusion.9
  188.6 0.7 copy.56.eocc_ref
  189.3 0.6 sub.49.ecol_ref
  189.9 0.9 copy-done.17
  191.1 18.0 %last_product.7 = f32[2048,1024]{1,0:T(8,128)} custom-call(s32[8]{0:T(128)S(1)} %copy-done.26, s32[8]{0:T(128)S(1)} %copy-done.30, s32[1]{0:T(128)} %get-tuple-element.163.win, s32[2]{0:T(128)S(1)} %get-tuple-element.164.at, s32[1]{0:T(128)} %bitcast.27.inner, bf16[4,2,640,1280]{3,2,1,0:T(8,128)(2,1)} %bitcast.74, bf16[640,640]{1,0:T(8,128)(2,1)} %get-tuple-element.177.t0, ...), custom_call_target="tpu_custom_call" | custom-call | flops 6710886400 | bytes 13762560 | tf_op jit(solution)/shard_map/cond/branch_3_fun/last_product/pallas_call | solution.py:342
  (53 shorter events, 3.7 us)
Async XLA Ops:
  9.4 2.3 %copy-start.26 = (s32[8]{0:T(128)S(1)}, s32[8]{0:T(128)}, u32[]{:S(2)}) copy-start(s32[8]{0:T(128)} %get-tuple-element.161.occ) | copy-start | bytes 100 | tf_op jit(solution)/shard_map/cond
  9.4 2.3 %copy-start.30 = (s32[8]{0:T(128)S(1)}, s32[8]{0:T(128)}, u32[]{:S(2)}) copy-start(s32[8]{0:T(128)} %get-tuple-element.162.virt) | copy-start | bytes 100 | tf_op jit(solution)/shard_map/cond
  11.2 50.8 %collective-permute-start.45 = (bf16[1024,1024]{1,0:T(8,128)(2,1)S(1)}, bf16[1024,1024]{1,0:T(8,128)(2,1)}, u32[]{:S(2)}, u32[]{:S(2)}) collective-permute-start(bf16[1024,1024]{1,0:T(8,128)(2,1)S(1)} %bitcast.77), channel_id=1, source_target_pairs={{0,1},{1,0},{2,3},{3,2},{4,5},{5,4},{6,7},{7,6},{8,9},{9,8},{10,11... | collective-permute-start | bytes 6291464 | tf_op jit(solution)/shard_map/cond/branch_3_fun/ppermute | solution.py:396
  56.8 23.8 %all-to-all-start.7 = ((bf16[8,128,640]{2,1,0:T(8,128)(2,1)}), bf16[8,128,640]{2,1,0:T(8,128)(2,1)S(1)}, u32[]{:S(2)}, u32[]{:S(2)}) async-start(bf16[8,128,640]{2,1,0:T(8,128)(2,1)} %get-tuple-element.169), calls=%async_computation.7 | async-start | bytes 2621440 | tf_op jit(solution)/shard_map/cond/branch_3_fun/all_to_all | solution.py:402
  60.4 102.9 %all-gather.15.cloned.1.call-start = ((), (), s32[]{:S(2)}) async-start(), calls=%async_computation.11 | async-start | bytes 14745600 | tf_op jit(solution)/shard_map/cond/branch_3_fun/all_gather | solution.py:412
  60.4 27.0 %collective-permute-start.46 = (bf16[640,640]{1,0:T(8,128)(2,1)}, bf16[640,640]{1,0:T(8,128)(2,1)}, u32[]{:S(2)}, u32[]{:S(2)}) collective-permute-start(bf16[640,640]{1,0:T(8,128)(2,1)} %get-tuple-element.172.awaited.refs_0_), channel_id=1, source_target_pairs={{0,8},{8,24},{24,16},{16,0},{1,9},{9,25},{25,17},{17,1},{2,10},{10... | collective-permute-start | bytes 2457608 | tf_op jit(solution)/shard_map/cond/branch_3_fun/ppermute | solution.py:399
  80.6 1.1 copy-start.11
  87.4 3.1 %copy-start.38 = (bf16[640,640]{1,0:T(8,128)(2,1)S(1)}, bf16[640,640]{1,0:T(8,128)(2,1)}, u32[]{:S(2)}) copy-start(bf16[640,640]{1,0:T(8,128)(2,1)} %get-tuple-element.172.awaited.refs_0_) | copy-start | bytes 2457604 | tf_op jit(solution)/shard_map/cond
  87.4 22.4 %collective-permute-start.49 = (bf16[640,640]{1,0:T(8,128)(2,1)}, bf16[640,640]{1,0:T(8,128)(2,1)}, u32[]{:S(2)}, u32[]{:S(2)}) collective-permute-start(bf16[640,640]{1,0:T(8,128)(2,1)} %get-tuple-element.176.refs_1_), channel_id=1, source_target_pairs={{0,8},{8,24},{24,16},{16,0},{1,9},{9,25},{25,17},{17,1},{2,10},{10... | collective-permute-start | bytes 2457608 | tf_op jit(solution)/shard_map/cond/branch_3_fun/ppermute | solution.py:399
  90.1 37.2 %collective-permute-start.47 = (bf16[640,640]{1,0:T(8,128)(2,1)}, bf16[640,640]{1,0:T(8,128)(2,1)S(1)}, u32[]{:S(2)}, u32[]{:S(2)}) collective-permute-start(bf16[640,640]{1,0:T(8,128)(2,1)} %collective-permute-done.46.refs_2_.refs_4_), channel_id=1, source_target_pairs={{0,8},{8,24},{24,16},{16,0},{1,9},{9,25},{25,17},{17,1},{2,10},{10... | collective-permute-start | bytes 2457608 | tf_op jit(solution)/shard_map/cond/branch_3_fun/ppermute | solution.py:399
  90.5 36.7 %collective-permute-start.52 = (bf16[640,640]{1,0:T(8,128)(2,1)S(1)}, bf16[640,640]{1,0:T(8,128)(2,1)S(1)}, u32[]{:S(2)}, u32[]{:S(2)}) collective-permute-start(bf16[640,640]{1,0:T(8,128)(2,1)S(1)} %copy-done.38), channel_id=1, source_target_pairs={{0,1},{1,0},{2,3},{3,2},{4,5},{5,4},{6,7},{7,6},{8,9},{9,8},{10,11... | collective-permute-start | bytes 2457608 | tf_op jit(solution)/shard_map/cond/branch_3_fun/ppermute | solution.py:396
  109.8 34.2 %collective-permute-start.50 = (bf16[640,640]{1,0:T(8,128)(2,1)}, bf16[640,640]{1,0:T(8,128)(2,1)}, u32[]{:S(2)}, u32[]{:S(2)}) collective-permute-start(bf16[640,640]{1,0:T(8,128)(2,1)} %collective-permute-done.49.refs_5_), channel_id=1, source_target_pairs={{0,8},{8,24},{24,16},{16,0},{1,9},{9,25},{25,17},{17,1},{2,10},{10... | collective-permute-start | bytes 2457608 | tf_op jit(solution)/shard_map/cond/branch_3_fun/ppermute | solution.py:399
  111.5 33.7 %collective-permute-start.54 = (bf16[640,640]{1,0:T(8,128)(2,1)}, bf16[640,640]{1,0:T(8,128)(2,1)}, u32[]{:S(2)}, u32[]{:S(2)}) collective-permute-start(bf16[640,640]{1,0:T(8,128)(2,1)} %collective-permute-done.46.refs_2_.refs_4_), channel_id=1, source_target_pairs={{0,1},{1,0},{2,3},{3,2},{4,5},{5,4},{6,7},{7,6},{8,9},{9,8},{10,11... | collective-permute-start | bytes 2457608 | tf_op jit(solution)/shard_map/cond/branch_3_fun/ppermute | solution.py:396
  111.5 35.4 %collective-permute-start.53 = (bf16[640,640]{1,0:T(8,128)(2,1)}, bf16[640,640]{1,0:T(8,128)(2,1)}, u32[]{:S(2)}, u32[]{:S(2)}) collective-permute-start(bf16[640,640]{1,0:T(8,128)(2,1)} %get-tuple-element.176.refs_1_), channel_id=1, source_target_pairs={{0,1},{1,0},{2,3},{3,2},{4,5},{5,4},{6,7},{7,6},{8,9},{9,8},{10,11... | collective-permute-start | bytes 2457608 | tf_op jit(solution)/shard_map/cond/branch_3_fun/ppermute | solution.py:396
  127.2 21.0 %copy-start.39 = (bf16[640,640]{1,0:T(8,128)(2,1)}, bf16[640,640]{1,0:T(8,128)(2,1)S(1)}, u32[]{:S(2)}) copy-start(bf16[640,640]{1,0:T(8,128)(2,1)S(1)} %collective-permute-done.47.refs_8_) | copy-start | bytes 2457604 | tf_op jit(solution)/shard_map/cond
  127.2 21.0 %collective-permute-start.56 = (bf16[640,640]{1,0:T(8,128)(2,1)S(1)}, bf16[640,640]{1,0:T(8,128)(2,1)}, u32[]{:S(2)}, u32[]{:S(2)}) collective-permute-start(bf16[640,640]{1,0:T(8,128)(2,1)S(1)} %collective-permute-done.47.refs_8_), channel_id=1, source_target_pairs={{0,1},{1,0},{2,3},{3,2},{4,5},{5,4},{6,7},{7,6},{8,9},{9,8},{10,11... | collective-permute-start | bytes 2457608 | tf_op jit(solution)/shard_map/cond/branch_3_fun/ppermute | solution.py:396
  127.2 0.9 copy-start.40
  128.2 20.0 %collective-permute-start.55 = (bf16[640,640]{1,0:T(8,128)(2,1)}, bf16[640,640]{1,0:T(8,128)(2,1)S(1)}, u32[]{:S(2)}, u32[]{:S(2)}) collective-permute-start(bf16[640,640]{1,0:T(8,128)(2,1)} %collective-permute-done.49.refs_5_), channel_id=1, source_target_pairs={{0,1},{1,0},{2,3},{3,2},{4,5},{5,4},{6,7},{7,6},{8,9},{9,8},{10,11... | collective-permute-start | bytes 2457608 | tf_op jit(solution)/shard_map/cond/branch_3_fun/ppermute | solution.py:396
  144.0 4.3 %collective-permute-start.57 = (bf16[640,640]{1,0:T(8,128)(2,1)}, bf16[640,640]{1,0:T(8,128)(2,1)}, u32[]{:S(2)}, u32[]{:S(2)}) collective-permute-start(bf16[640,640]{1,0:T(8,128)(2,1)} %collective-permute-done.50.refs_9_), channel_id=1, source_target_pairs={{0,1},{1,0},{2,3},{3,2},{4,5},{5,4},{6,7},{7,6},{8,9},{9,8},{10,11... | collective-permute-start | bytes 2457608 | tf_op jit(solution)/shard_map/cond/branch_3_fun/ppermute | solution.py:396
  145.2 36.2 %collective-permute-start.48 = (bf16[640,640]{1,0:T(8,128)(2,1)S(1)}, bf16[640,640]{1,0:T(8,128)(2,1)S(1)}, u32[]{:S(2)}, u32[]{:S(2)}) collective-permute-start(bf16[640,640]{1,0:T(8,128)(2,1)S(1)} %collective-permute-done.47.refs_8_), channel_id=1, source_target_pairs={{0,8},{8,24},{24,16},{16,0},{1,9},{9,25},{25,17},{17,1},{2,10},{10... | collective-permute-start | bytes 2457608 | tf_op jit(solution)/shard_map/cond/branch_3_fun/ppermute | solution.py:399
  146.9 37.4 %collective-permute-start.51 = (bf16[640,640]{1,0:T(8,128)(2,1)}, bf16[640,640]{1,0:T(8,128)(2,1)S(1)}, u32[]{:S(2)}, u32[]{:S(2)}) collective-permute-start(bf16[640,640]{1,0:T(8,128)(2,1)} %collective-permute-done.50.refs_9_), channel_id=1, source_target_pairs={{0,8},{8,24},{24,16},{16,0},{1,9},{9,25},{25,17},{17,1},{2,10},{10... | collective-permute-start | bytes 2457608 | tf_op jit(solution)/shard_map/cond/branch_3_fun/ppermute | solution.py:399
  148.2 1.0 copy-start.41
  181.4 5.6 %copy-start.22 = (f32[8,64]{1,0:T(8,128)S(1)}, f32[8,64]{1,0:T(8,128)}, u32[]{:S(2)}) copy-start(f32[8,64]{1,0:T(8,128)} %get-tuple-element.348) | copy-start | bytes 6148 | tf_op jit(solution)/shard_map/cond
  181.4 2.9 %copy-start.2 = (bf16[640,640]{1,0:T(8,128)(2,1)}, bf16[640,640]{1,0:T(8,128)(2,1)S(1)}, u32[]{:S(2)}) copy-start(bf16[640,640]{1,0:T(8,128)(2,1)S(1)} %collective-permute-done.48.refs_0_) | copy-start | bytes 2457604 | tf_op jit(solution)/shard_map/cond
  184.3 0.9 copy-start.3
  185.2 4.7 %collective-permute-start.58 = (bf16[640,640]{1,0:T(8,128)(2,1)}, bf16[640,640]{1,0:T(8,128)(2,1)S(1)}, u32[]{:S(2)}, u32[]{:S(2)}) collective-permute-start(bf16[640,640]{1,0:T(8,128)(2,1)} %get-tuple-element.177.t0), channel_id=1, source_target_pairs={{0,1},{1,0},{2,3},{3,2},{4,5},{5,4},{6,7},{7,6},{8,9},{9,8},{10,11... | collective-permute-start | bytes 2457608 | tf_op jit(solution)/shard_map/cond/branch_3_fun/ppermute | solution.py:396
  185.2 4.7 %collective-permute-start.59 = (bf16[640,640]{1,0:T(8,128)(2,1)}, bf16[640,640]{1,0:T(8,128)(2,1)S(1)}, u32[]{:S(2)}, u32[]{:S(2)}) collective-permute-start(bf16[640,640]{1,0:T(8,128)(2,1)} %get-tuple-element.178.t1), channel_id=1, source_target_pairs={{0,1},{1,0},{2,3},{3,2},{4,5},{5,4},{6,7},{7,6},{8,9},{9,8},{10,11... | collective-permute-start | bytes 2457608 | tf_op jit(solution)/shard_map/cond/branch_3_fun/ppermute | solution.py:396
  189.9 0.9 copy-start.17
  189.9 1.2 copy-start.18
Sparse Core Ops, SparseCore 0:
  87.5 74.8 all-gather.14
where the time goes:
time: 216 us
  Pallas kernels  97.1 us (45%)
  waiting for transfers between devices  52.8 us (24%)
  blocking collectives  23.6 us (11%)
  starting transfers between devices  15.1 us (7%)
  between operations  14.7 us (7%)
  local copies, waits for them, and re-layouts  10.9 us (5%)
    ppermute x6, waiting for transfers between devices, around(): return lax.ppermute(x, 'row', ring)  52.8 us
    all_to_all x1, blocking collectives, exchange(): return lax.all_to_all(x, 'col', split_axis=0, concat_axis=0, tiled=True)  23.6 us
    pallas_call x1, Pallas kernels, compact_ints(): pl.pallas_call(functools.partial(ints_kernel, rows, cols), out_shape=jax....  18.5 us
    pallas_call x1, Pallas kernels, product(): pl.pallas_call(product_kernel, out_shape=jax.ShapeDtypeStruct((2, rows, B...  18.2 us
    pallas_call x1, Pallas kernels, last(): pl.pallas_call(functools.partial(last_kernel, rows, cols), out_shape=jax....  18 us
    pallas_call x1, Pallas kernels, prep(): pl.pallas_call(functools.partial(prep_kernel, size), out_shape=(shape, sh...  15.7 us
    pallas_call x1, Pallas kernels, widen(): pl.pallas_call(functools.partial(widen_kernel, rows, cols, slots), out_sh...  14 us
    pallas_call x2, Pallas kernels, compact_rows(): pl.pallas_call(functools.partial(rows_kernel, rows, parity, len(passed) +...  11.5 us
  transfers between devices with their start and end apart: 17, of which 4 were waited for; matrix products, arithmetic and copies ran while one was open for 2% of the time, Pallas kernels for 36%

commit v1 on v0

--- a/solution.py
+++ b/solution.py
@@ -55,7 +55,7 @@
     return jnp.dot(a, b, preferred_element_type=F32)
 
 
-def prep_kernel(size, occ, virt, win, t2_ref, even_ref, odd_ref, x_ref):
+def prep_kernel(size, occ, virt, win, t2_ref, even_ref, odd_ref, x_ref, acc_ref):
     counts = pair_scalars(occ, virt, win, pl.program_id(0))
     row = iota((256, 1), 0)
     source = (((row >> 6) & 1) << 7) | (((row >> 2) & 15) << 3) | ((row & 3) << 1) | (row >> 7)
@@ -73,15 +73,34 @@
             p, q = 4 * group + (r >> 6), r & 63
             spot = place(q, p, half == 1, counts)
             targets.append(jnp.where(spot >= 0, spot + (q & 1) * size, -1))
+    (o_a, o_b), (v_a, v_b), (start_even, start_odd) = counts
+
     @pl.loop(0, 2)
     def _(core):
+        start = jnp.where(core == 0, start_even, start_odd)
+        end = start + o_b * ((v_b + 1 - core) >> 1)
         for tile in range(-(-size // 256)):
             col = min(256 * tile, size - 256)
             lane = iota((256, 256), 1) + (col + core * size)
-            acc = jnp.zeros((256, 256), F32)
-            for chunk in range(4 if col >= BLOCK // 2 else 0, 8):
-                acc += dot(x_ref[:, chunk * 256 : chunk * 256 + 256], one_hot(targets[chunk], lane))
-            acc = acc.astype(BF16)
+
+            def part(half):
+                chunks = range(4 * half, 4 * half + 4)
+                return sum(
+                    dot(x_ref[:, c * 256 : c * 256 + 256], one_hot(targets[c], lane)) for c in chunks
+                )
+
+            acc_ref[...] = jnp.zeros((256, 256), F32)
+            if col < BLOCK // 2:
+
+                @pl.when(start > col)
+                def _():
+                    acc_ref[...] += part(0)
+
+            @pl.when((start < col + 256) & (end > col))
+            def _():
+                acc_ref[...] += part(1)
+
+            acc = acc_ref[...].astype(BF16)
             even_ref[core, :, col : col + 256] = acc[:128]
             odd_ref[core, :, col : col + 256] = acc[128:]
 
@@ -99,7 +118,7 @@
                 pl.BlockSpec((2, 2, OCC_CAP, OCC_CAP, 8, VIR_CAP), lambda k, *_: (0, k, 0, 0, 0, 0))
             ],
             out_specs=[block, block],
-            scratch_shapes=[pltpu.VMEM((256, 2048), BF16)],
+            scratch_shapes=[pltpu.VMEM((256, 2048), BF16), pltpu.VMEM((256, 256), F32)],
         ),
         compiler_params=params(),
         cost_estimate=cost(2 * 4 * 256 * 2048 * 2 * size, 12 * 2**20),

time: 216 us -> 422 us (1.95); the launches traced: 216 us -> 417 us
  waiting for transfers between devices: 52.8 us -> 199 us
  Pallas kernels: 97.1 us -> 151 us
  blocking collectives: 23.6 us -> 0 us
  loops' own time: 1.04 us -> 16.6 us
  starting transfers between devices: 15.1 us -> 21.3 us
    ppermute x6, waiting for transfers between devices: 52.8 us -> 173 us  [around(): return lax.ppermute(x, 'row', ring)]
    all_to_all x1 -> x0, blocking collectives: 23.6 us -> none  [exchange(): return lax.all_to_all(x, 'col', split_axis=0, concat_axis=0, tiled=True)]
    all_to_all x1 -> x2, waiting for transfers between devices: 0.01 us -> 22.9 us  [exchange(): return lax.all_to_all(x, 'col', split_axis=0, concat_axis=0, tiled=True)]
    pallas_call x1, Pallas kernels: 18.2 us -> 36.7 us  [product(): pl.pallas_call(product_kernel, out_shape=jax.ShapeDtypeStruct((2, rows, B...]
    another operation x1, loops' own time: 1.04 us -> 16.6 us  [live_device(): lax.switch(index, [functools.partial(branch, size, nrow, ncol) for size i...]
    pallas_call x1, Pallas kernels: 18.5 us -> 28.8 us  [compact_ints(): pl.pallas_call(functools.partial(ints_kernel, rows, cols), out_shape=jax....]
    pallas_call x1, Pallas kernels: 18 us -> 27.7 us  [last(): pl.pallas_call(functools.partial(last_kernel, rows, cols), out_shape=jax....]
    pallas_call x1, Pallas kernels: 14 us -> 21.1 us  [widen(): pl.pallas_call(functools.partial(widen_kernel, rows, cols, slots), out_sh...]
  transfers between devices with their start and end apart: 17 -> 18, of which waited for: 4 -> 8; matrix products, arithmetic and copies ran while one was open for 2% -> 2% of each run, Pallas kernels for 36% -> 25%
where the time goes in v1:
time: 422 us; the launch traced here: 417 us
  waiting for transfers between devices  199 us (47%)
  Pallas kernels  151 us (36%)
  starting transfers between devices  21.3 us (5%)
  loops' own time  16.6 us (4%)
  between operations  15 us (4%)
  local copies, waits for them, and re-layouts  13 us (3%)
    ppermute x6, waiting for transfers between devices, around(): return lax.ppermute(x, 'row', ring)  173 us
    pallas_call x1, Pallas kernels, product(): pl.pallas_call(product_kernel, out_shape=jax.ShapeDtypeStruct((2, rows, B...  36.7 us
    pallas_call x1, Pallas kernels, compact_ints(): pl.pallas_call(functools.partial(ints_kernel, rows, cols), out_shape=jax....  28.8 us
    pallas_call x1, Pallas kernels, last(): pl.pallas_call(functools.partial(last_kernel, rows, cols), out_shape=jax....  27.7 us
    all_to_all x2, waiting for transfers between devices, exchange(): return lax.all_to_all(x, 'col', split_axis=0, concat_axis=0, tiled=True)  22.9 us
    pallas_call x1, Pallas kernels, widen(): pl.pallas_call(functools.partial(widen_kernel, rows, cols, slots), out_sh...  21.1 us
    pallas_call x1, Pallas kernels, prep(): pl.pallas_call(functools.partial(prep_kernel, size), out_shape=(shape, sh...  19 us
    pallas_call x2, Pallas kernels, compact_rows(): pl.pallas_call(functools.partial(rows_kernel, rows, parity, len(passed) +...  16.7 us
  transfers between devices with their start and end apart: 18, of which 8 were waited for; matrix products, arithmetic and copies ran while one was open for 2% of the time, Pallas kernels for 25%

profile of v1, /device:TPU:0, one launch (start us, length us, event | category | flops | bytes accessed | tf_op | source)
XLA Modules:
  0.0 416.8 jit_solution(8568040888685925526)
XLA Ops:
  7.3 1.2 choose.1
  9.1 400.5 %conditional.1 = (f32[2048,1024]{1,0:T(8,128)}) conditional(s32[]{:T(128)} %bitcast.36, ((), s32[8]{0:T(128)}, s32[8]{0:T(128)}, s32[1]{0:T(128)}, bf16[2,8,16,16,8,64]{5,4,3,2,1,0:T(8,128)(2,1)}, /*index=5*/s32[2]{0:T(128)S(1)}, bf16[2048,1024]{1,0:T(8,128)(2,1)}, s32[]{:T(128)}, f32[8,64]{1,0:T(8,128)}, ...), branch_computations={%region_0.1_spmd, %region_1.2_spmd, %region_2.3_spmd, %region_3.4_... | conditional | flops 115964116992 | bytes 415283904 | solution.py:480
  9.2 19.0 %prep_amplitudes.4 = (bf16[8,128,1024]{2,1,0:T(8,128)(2,1)}, bf16[8,128,1024]{2,1,0:T(8,128)(2,1)}) custom-call(s32[8]{0:T(128)} %get-tuple-element.96.occ, s32[8]{0:T(128)} %get-tuple-element.98.virt, s32[1]{0:T(128)} %get-tuple-element.100.win, bf16[2,8,16,16,8,64]{5,4,3,2,1,0:T(8,128)(2,1)} %get-tuple-element.219.t2_ref), custom_call_target="tpu_custom_call" | custom-call | flops 8589934592 | bytes 12582912 | tf_op jit(solution)/shard_map/cond/branch_0_fun/prep_amplitudes/pallas_call | solution.py:111
  28.2 5.2 %all-to-all-start = ((bf16[8,128,1024]{2,1,0:T(8,128)(2,1)}), bf16[8,128,1024]{2,1,0:T(8,128)(2,1)S(1)}, u32[]{:S(2)}, u32[]{:S(2)}) async-start(bf16[8,128,1024]{2,1,0:T(8,128)(2,1)} %get-tuple-element.104), calls=%async_computation | async-start | bytes 4194304 | tf_op jit(solution)/shard_map/cond/branch_0_fun/all_to_all | solution.py:421
  33.4 3.2 constant_dynamic-slice_fusion.4
  37.1 22.9 %all-to-all-done.x_ref = bf16[8,128,1024]{2,1,0:T(8,128)(2,1)S(1)} async-done(((bf16[8,128,1024]{2,1,0:T(8,128)(2,1)}), bf16[8,128,1024]{2,1,0:T(8,128)(2,1)S(1)}, u32[]{:S(2)}, u32[]{:S(2)}) %all-to-all-start) | async-done | bytes 2097184 | tf_op jit(solution)/shard_map/cond/branch_0_fun/all_to_all | solution.py:421
  60.0 1.3 copy-done.4
  61.3 8.3 %compact_rows.8 = (bf16[1024,1024]{1,0:T(8,128)(2,1)}, bf16[8,128,1024]{2,1,0:T(8,128)(2,1)}) custom-call(s32[8]{0:T(128)S(1)} %copy-done.23, s32[8]{0:T(128)S(1)} %copy-done.27, s32[1]{0:T(128)} %get-tuple-element.100.win, s32[2]{0:T(128)S(1)} %get-tuple-element.101.at, bf16[8,128,1024]{2,1,0:T(8,128)(2,1)} %copy-done.4, ...), custom_call_target="tpu_custom_call", output_to_operand_aliasing={{1}: (5, {})} | custom-call | flops 4294967296 | bytes 4194304 | tf_op jit(solution)/shard_map/cond/branch_0_fun/compact_rows/pallas_call | solution.py:158
  69.7 3.6 all-to-all-start.1
  73.3 1.6 collective-permute-start.1
  75.0 28.8 %compact_ints.4.refs_0_ = bf16[1024,2048]{1,0:T(8,128)(2,1)} custom-call(s32[8]{0:T(128)S(1)} %copy-done.23, s32[8]{0:T(128)S(1)} %copy-done.27, s32[1]{0:T(128)} %get-tuple-element.100.win, s32[2]{0:T(128)S(1)} %get-tuple-element.101.at, bf16[2,32,2,16,1024]{4,3,2,1,0:T(8,128)(2,1)} %bitcast.66, bf16[1024,1024]{1,0:T(8,128)(2,1)} %collective-permute-done.other_ref, ...), custom_call_target="tpu_custom_call" | custom-call | flops 17179869184 | bytes 8388608 | tf_op jit(solution)/shard_map/cond/branch_0_fun/compact_ints/pallas_call | solution.py:213
  103.7 1.4 copy-done.5
  105.1 8.4 %compact_rows.9 = (bf16[1024,1024]{1,0:T(8,128)(2,1)}, bf16[1024,2048]{1,0:T(8,128)(2,1)}) custom-call(s32[8]{0:T(128)S(1)} %copy-done.23, s32[8]{0:T(128)S(1)} %copy-done.27, s32[1]{0:T(128)} %get-tuple-element.100.win, s32[2]{0:T(128)S(1)} %get-tuple-element.101.at, bf16[8,128,1024]{2,1,0:T(8,128)(2,1)} %copy-done.5, ...), custom_call_target="tpu_custom_call", output_to_operand_aliasing={{1}: (5, {})} | custom-call | flops 4294967296 | bytes 4194304 | tf_op jit(solution)/shard_map/cond/branch_0_fun/compact_rows/pallas_call | solution.py:158
  113.5 8.9 %collective-permute-done.1.refs_2_.refs_4_ = bf16[1024,1024]{1,0:T(8,128)(2,1)} collective-permute-done((bf16[1024,1024]{1,0:T(8,128)(2,1)}, bf16[1024,1024]{1,0:T(8,128)(2,1)}, u32[]{:S(2)}, u32[]{:S(2)}) %collective-permute-start.1) | collective-permute-done | bytes 2097184 | tf_op jit(solution)/shard_map/cond/branch_0_fun/ppermute | solution.py:418
  122.5 1.6 copy-done.7
  124.0 0.8 collective-permute-start.4
  124.8 3.4 collective-permute-start.2
  128.2 45.4 %collective-permute-done.4.refs_5_ = bf16[1024,1024]{1,0:T(8,128)(2,1)} collective-permute-done((bf16[1024,1024]{1,0:T(8,128)(2,1)S(1)}, bf16[1024,1024]{1,0:T(8,128)(2,1)}, u32[]{:S(2)}, u32[]{:S(2)}) %collective-permute-start.4) | collective-permute-done | bytes 2097184 | tf_op jit(solution)/shard_map/cond/branch_0_fun/ppermute | solution.py:418
  173.6 0.7 collective-permute-start.5
  174.8 43.7 %collective-permute-done.2.refs_8_ = bf16[1024,1024]{1,0:T(8,128)(2,1)} collective-permute-done((bf16[1024,1024]{1,0:T(8,128)(2,1)}, bf16[1024,1024]{1,0:T(8,128)(2,1)}, u32[]{:S(2)}, u32[]{:S(2)}) %collective-permute-start.2) | collective-permute-done | bytes 2097184 | tf_op jit(solution)/shard_map/cond/branch_0_fun/ppermute | solution.py:418
  218.5 43.4 %collective-permute-done.5.refs_9_ = bf16[1024,1024]{1,0:T(8,128)(2,1)} collective-permute-done((bf16[1024,1024]{1,0:T(8,128)(2,1)}, bf16[1024,1024]{1,0:T(8,128)(2,1)}, u32[]{:S(2)}, u32[]{:S(2)}) %collective-permute-start.5) | collective-permute-done | bytes 2097184 | tf_op jit(solution)/shard_map/cond/branch_0_fun/ppermute | solution.py:418
  263.2 0.8 collective-permute-start.3
  264.0 3.7 collective-permute-start.6
  267.7 21.1 %widen.4.wide_ref = bf16[3,2048,1024]{2,1,0:T(8,128)(2,1)} custom-call(s32[8]{0:T(128)S(1)} %copy-done.23, s32[8]{0:T(128)S(1)} %copy-done.27, s32[1]{0:T(128)} %get-tuple-element.100.win, s32[2]{0:T(128)S(1)} %get-tuple-element.101.at, bf16[1024,1024]{1,0:T(8,128)(2,1)} %get-tuple-element.109.awaited.refs_0_, ...), custom_call_target="tpu_custom_call" | custom-call | flops 12884901888 | bytes 37748736 | tf_op jit(solution)/shard_map/cond/branch_0_fun/widen/pallas_call | solution.py:267
  288.8 36.7 %product.4.refs_2_.old_ref = f32[2,1024,1024]{2,1,0:T(8,128)} custom-call(s32[3]{0:T(128)} %slice_bitcast_fusion.inner, bf16[4,2,1024,2048]{3,2,1,0:T(8,128)(2,1)} %bitcast.78, bf16[3,2048,1024]{2,1,0:T(8,128)(2,1)} %widen.4.wide_ref), custom_call_target="tpu_custom_call" | custom-call | flops 51539607552 | bytes 25165824 | tf_op jit(solution)/shard_map/cond/branch_0_fun/product/pallas_call | solution.py:296
  325.5 31.9 %collective-permute-done.6.refs_1_ = bf16[1024,1024]{1,0:T(8,128)(2,1)} collective-permute-done((bf16[1024,1024]{1,0:T(8,128)(2,1)}, bf16[1024,1024]{1,0:T(8,128)(2,1)}, u32[]{:S(2)}, u32[]{:S(2)}) %collective-permute-start.6) | collective-permute-done | bytes 2097184 | tf_op jit(solution)/shard_map/cond/branch_0_fun/ppermute | solution.py:418
  359.4 0.7 fusion.1
  360.2 0.7 fusion
  360.9 0.7 copy.53.eocc_ref
  362.2 2.6 collective-permute-done.13.s0
  364.9 1.2 copy-done.31
  366.1 27.7 %last_product.4 = f32[2048,1024]{1,0:T(8,128)} custom-call(s32[8]{0:T(128)S(1)} %copy-done.23, s32[8]{0:T(128)S(1)} %copy-done.27, s32[1]{0:T(128)} %get-tuple-element.100.win, s32[2]{0:T(128)S(1)} %get-tuple-element.101.at, s32[1]{0:T(128)} %bitcast.inner, bf16[4,2,1024,2048]{3,2,1,0:T(8,128)(2,1)} %bitcast.79, bf16[1024,1024]{1,0:T(8,128)(2,1)} %get-tuple-element.114.t0, ...), custom_call_target="tpu_custom_call" | custom-call | flops 17179869184 | bytes 25165824 | tf_op jit(solution)/shard_map/cond/branch_0_fun/last_product/pallas_call | solution.py:361
  (46 shorter events, 4.7 us)
Async XLA Ops:
  28.2 31.8 %all-to-all-start = ((bf16[8,128,1024]{2,1,0:T(8,128)(2,1)}), bf16[8,128,1024]{2,1,0:T(8,128)(2,1)S(1)}, u32[]{:S(2)}, u32[]{:S(2)}) async-start(bf16[8,128,1024]{2,1,0:T(8,128)(2,1)} %get-tuple-element.104), calls=%async_computation | async-start | bytes 4194304 | tf_op jit(solution)/shard_map/cond/branch_0_fun/all_to_all | solution.py:421
  33.4 28.0 %copy-start.23 = (s32[8]{0:T(128)S(1)}, s32[8]{0:T(128)}, u32[]{:S(2)}) copy-start(s32[8]{0:T(128)} %get-tuple-element.96.occ) | copy-start | bytes 100 | tf_op jit(solution)/shard_map/cond
  33.4 28.0 %copy-start.27 = (s32[8]{0:T(128)S(1)}, s32[8]{0:T(128)}, u32[]{:S(2)}) copy-start(s32[8]{0:T(128)} %get-tuple-element.98.virt) | copy-start | bytes 100 | tf_op jit(solution)/shard_map/cond
  36.6 38.4 %collective-permute-start = (bf16[1024,1024]{1,0:T(8,128)(2,1)}, bf16[1024,1024]{1,0:T(8,128)(2,1)}, u32[]{:S(2)}, u32[]{:S(2)}) collective-permute-start(bf16[1024,1024]{1,0:T(8,128)(2,1)} %bitcast.2), channel_id=1, source_target_pairs={{0,1},{1,0},{2,3},{3,2},{4,5},{5,4},{6,7},{7,6},{8,9},{9,8},{10,11... | collective-permute-start | bytes 6291464 | tf_op jit(solution)/shard_map/cond/branch_0_fun/ppermute | solution.py:415
  60.0 1.3 copy-start.4
  69.7 34.1 %all-to-all-start.1 = ((bf16[8,128,1024]{2,1,0:T(8,128)(2,1)}), bf16[8,128,1024]{2,1,0:T(8,128)(2,1)S(1)}, u32[]{:S(2)}, u32[]{:S(2)}) async-start(bf16[8,128,1024]{2,1,0:T(8,128)(2,1)} %get-tuple-element.106), calls=%async_computation.1 | async-start | bytes 4194304 | tf_op jit(solution)/shard_map/cond/branch_0_fun/all_to_all | solution.py:421
  73.3 215.5 %all-gather.9.cloned.1.call-start = ((), (), s32[]{:S(2)}) async-start(), calls=%async_computation.8 | async-start | bytes 37748736 | tf_op jit(solution)/shard_map/cond/branch_0_fun/all_gather | solution.py:431
  73.3 49.1 %collective-permute-start.1 = (bf16[1024,1024]{1,0:T(8,128)(2,1)}, bf16[1024,1024]{1,0:T(8,128)(2,1)}, u32[]{:S(2)}, u32[]{:S(2)}) collective-permute-start(bf16[1024,1024]{1,0:T(8,128)(2,1)} %get-tuple-element.109.awaited.refs_0_), channel_id=1, source_target_pairs={{0,8},{8,24},{24,16},{16,0},{1,9},{9,25},{25,17},{17,1},{2,10},{10... | collective-permute-start | bytes 6291464 | tf_op jit(solution)/shard_map/cond/branch_0_fun/ppermute | solution.py:418
  103.7 1.4 copy-start.5
  122.4 1.6 copy-start.7
  124.0 49.6 %collective-permute-start.4 = (bf16[1024,1024]{1,0:T(8,128)(2,1)S(1)}, bf16[1024,1024]{1,0:T(8,128)(2,1)}, u32[]{:S(2)}, u32[]{:S(2)}) collective-permute-start(bf16[1024,1024]{1,0:T(8,128)(2,1)S(1)} %copy-done.7), channel_id=1, source_target_pairs={{0,8},{8,24},{24,16},{16,0},{1,9},{9,25},{25,17},{17,1},{2,10},{10... | collective-permute-start | bytes 6291464 | tf_op jit(solution)/shard_map/cond/branch_0_fun/ppermute | solution.py:418
  124.8 50.0 %collective-permute-start.7 = (bf16[1024,1024]{1,0:T(8,128)(2,1)}, bf16[1024,1024]{1,0:T(8,128)(2,1)}, u32[]{:S(2)}, u32[]{:S(2)}) collective-permute-start(bf16[1024,1024]{1,0:T(8,128)(2,1)} %get-tuple-element.109.awaited.refs_0_), channel_id=1, source_target_pairs={{0,1},{1,0},{2,3},{3,2},{4,5},{5,4},{6,7},{7,6},{8,9},{9,8},{10,11... | collective-permute-start | bytes 6291464 | tf_op jit(solution)/shard_map/cond/branch_0_fun/ppermute | solution.py:415
  124.8 93.7 %collective-permute-start.2 = (bf16[1024,1024]{1,0:T(8,128)(2,1)}, bf16[1024,1024]{1,0:T(8,128)(2,1)}, u32[]{:S(2)}, u32[]{:S(2)}) collective-permute-start(bf16[1024,1024]{1,0:T(8,128)(2,1)} %collective-permute-done.1.refs_2_.refs_4_), channel_id=1, source_target_pairs={{0,8},{8,24},{24,16},{16,0},{1,9},{9,25},{25,17},{17,1},{2,10},{10... | collective-permute-start | bytes 6291464 | tf_op jit(solution)/shard_map/cond/branch_0_fun/ppermute | solution.py:418
  173.6 88.3 %collective-permute-start.5 = (bf16[1024,1024]{1,0:T(8,128)(2,1)}, bf16[1024,1024]{1,0:T(8,128)(2,1)}, u32[]{:S(2)}, u32[]{:S(2)}) collective-permute-start(bf16[1024,1024]{1,0:T(8,128)(2,1)} %collective-permute-done.4.refs_5_), channel_id=1, source_target_pairs={{0,8},{8,24},{24,16},{16,0},{1,9},{9,25},{25,17},{17,1},{2,10},{10... | collective-permute-start | bytes 6291464 | tf_op jit(solution)/shard_map/cond/branch_0_fun/ppermute | solution.py:418
  174.3 88.9 %collective-permute-start.8 = (bf16[1024,1024]{1,0:T(8,128)(2,1)S(1)}, bf16[1024,1024]{1,0:T(8,128)(2,1)}, u32[]{:S(2)}, u32[]{:S(2)}) collective-permute-start(bf16[1024,1024]{1,0:T(8,128)(2,1)S(1)} %copy-done.7), channel_id=1, source_target_pairs={{0,1},{1,0},{2,3},{3,2},{4,5},{5,4},{6,7},{7,6},{8,9},{9,8},{10,11... | collective-permute-start | bytes 6291464 | tf_op jit(solution)/shard_map/cond/branch_0_fun/ppermute | solution.py:415
  174.3 89.7 %collective-permute-start.9 = (bf16[1024,1024]{1,0:T(8,128)(2,1)}, bf16[1024,1024]{1,0:T(8,128)(2,1)}, u32[]{:S(2)}, u32[]{:S(2)}) collective-permute-start(bf16[1024,1024]{1,0:T(8,128)(2,1)} %collective-permute-done.1.refs_2_.refs_4_), channel_id=1, source_target_pairs={{0,1},{1,0},{2,3},{3,2},{4,5},{5,4},{6,7},{7,6},{8,9},{9,8},{10,11... | collective-permute-start | bytes 6291464 | tf_op jit(solution)/shard_map/cond/branch_0_fun/ppermute | solution.py:415
  174.8 92.9 %collective-permute-start.10 = (bf16[1024,1024]{1,0:T(8,128)(2,1)}, bf16[1024,1024]{1,0:T(8,128)(2,1)}, u32[]{:S(2)}, u32[]{:S(2)}) collective-permute-start(bf16[1024,1024]{1,0:T(8,128)(2,1)} %collective-permute-done.4.refs_5_), channel_id=1, source_target_pairs={{0,1},{1,0},{2,3},{3,2},{4,5},{5,4},{6,7},{7,6},{8,9},{9,8},{10,11... | collective-permute-start | bytes 6291464 | tf_op jit(solution)/shard_map/cond/branch_0_fun/ppermute | solution.py:415
  218.5 49.2 %collective-permute-start.11 = (bf16[1024,1024]{1,0:T(8,128)(2,1)}, bf16[1024,1024]{1,0:T(8,128)(2,1)}, u32[]{:S(2)}, u32[]{:S(2)}) collective-permute-start(bf16[1024,1024]{1,0:T(8,128)(2,1)} %collective-permute-done.2.refs_8_), channel_id=1, source_target_pairs={{0,1},{1,0},{2,3},{3,2},{4,5},{5,4},{6,7},{7,6},{8,9},{9,8},{10,11... | collective-permute-start | bytes 6291464 | tf_op jit(solution)/shard_map/cond/branch_0_fun/ppermute | solution.py:415
  261.9 5.8 %collective-permute-start.12 = (bf16[1024,1024]{1,0:T(8,128)(2,1)}, bf16[1024,1024]{1,0:T(8,128)(2,1)}, u32[]{:S(2)}, u32[]{:S(2)}) collective-permute-start(bf16[1024,1024]{1,0:T(8,128)(2,1)} %collective-permute-done.5.refs_9_), channel_id=1, source_target_pairs={{0,1},{1,0},{2,3},{3,2},{4,5},{5,4},{6,7},{7,6},{8,9},{9,8},{10,11... | collective-permute-start | bytes 6291464 | tf_op jit(solution)/shard_map/cond/branch_0_fun/ppermute | solution.py:415
  263.2 62.3 %collective-permute-start.3 = (bf16[1024,1024]{1,0:T(8,128)(2,1)}, bf16[1024,1024]{1,0:T(8,128)(2,1)S(1)}, u32[]{:S(2)}, u32[]{:S(2)}) collective-permute-start(bf16[1024,1024]{1,0:T(8,128)(2,1)} %collective-permute-done.2.refs_8_), channel_id=1, source_target_pairs={{0,8},{8,24},{24,16},{16,0},{1,9},{9,25},{25,17},{17,1},{2,10},{10... | collective-permute-start | bytes 6291464 | tf_op jit(solution)/shard_map/cond/branch_0_fun/ppermute | solution.py:418
  264.0 93.4 %collective-permute-start.6 = (bf16[1024,1024]{1,0:T(8,128)(2,1)}, bf16[1024,1024]{1,0:T(8,128)(2,1)}, u32[]{:S(2)}, u32[]{:S(2)}) collective-permute-start(bf16[1024,1024]{1,0:T(8,128)(2,1)} %collective-permute-done.5.refs_9_), channel_id=1, source_target_pairs={{0,8},{8,24},{24,16},{16,0},{1,9},{9,25},{25,17},{17,1},{2,10},{10... | collective-permute-start | bytes 6291464 | tf_op jit(solution)/shard_map/cond/branch_0_fun/ppermute | solution.py:418
  325.5 33.8 %copy-start.19 = (f32[8,64]{1,0:T(8,128)S(1)}, f32[8,64]{1,0:T(8,128)}, u32[]{:S(2)}) copy-start(f32[8,64]{1,0:T(8,128)} %get-tuple-element.339) | copy-start | bytes 6148 | tf_op jit(solution)/shard_map/cond
  325.5 31.9 %copy-start.6 = (bf16[1024,1024]{1,0:T(8,128)(2,1)}, bf16[1024,1024]{1,0:T(8,128)(2,1)S(1)}, u32[]{:S(2)}) copy-start(bf16[1024,1024]{1,0:T(8,128)(2,1)S(1)} %collective-permute-done.3.refs_0_) | copy-start | bytes 6291460 | tf_op jit(solution)/shard_map/cond
  357.4 7.3 %collective-permute-start.13 = (bf16[1024,1024]{1,0:T(8,128)(2,1)}, bf16[1024,1024]{1,0:T(8,128)(2,1)S(1)}, u32[]{:S(2)}, u32[]{:S(2)}) collective-permute-start(bf16[1024,1024]{1,0:T(8,128)(2,1)} %get-tuple-element.114.t0), channel_id=1, source_target_pairs={{0,1},{1,0},{2,3},{3,2},{4,5},{5,4},{6,7},{7,6},{8,9},{9,8},{10,11... | collective-permute-start | bytes 6291464 | tf_op jit(solution)/shard_map/cond/branch_0_fun/ppermute | solution.py:415
  357.4 7.5 %collective-permute-start.14 = (bf16[1024,1024]{1,0:T(8,128)(2,1)}, bf16[1024,1024]{1,0:T(8,128)(2,1)}, u32[]{:S(2)}, u32[]{:S(2)}) collective-permute-start(bf16[1024,1024]{1,0:T(8,128)(2,1)} %get-tuple-element.115.t1), channel_id=1, source_target_pairs={{0,1},{1,0},{2,3},{3,2},{4,5},{5,4},{6,7},{7,6},{8,9},{9,8},{10,11... | collective-permute-start | bytes 6291464 | tf_op jit(solution)/shard_map/cond/branch_0_fun/ppermute | solution.py:415
  364.7 1.4 copy-start.31
Sparse Core Ops, SparseCore 0:
  122.6 162.1 all-gather.8

commit v2 on v0

--- a/solution.py
+++ b/solution.py
@@ -126,12 +126,7 @@
     @pl.loop(0, -(-cols // 256))
     def _(n):
         lanes = pl.ds(pl.multiple_of(jnp.minimum(n * 256, cols - 256), 128), 256)
-        x = x_ref[:, :, lanes].reshape(BLOCK, 256)
-
-        @pl.loop(0, 2)
-        def _(half):
-            at_rows = pl.ds(pl.multiple_of(half * (rows // 2), 64), rows // 2)
-            out_ref[at_rows, lanes] = dot(sel_ref[at_rows, :], x).astype(BF16)
+        out_ref[:, lanes] = dot(sel_ref[...], x_ref[:, :, lanes].reshape(BLOCK, 256)).astype(BF16)
 
 
 def compact_rows(rows, cols, parity, scalars, at, x, passed=(), awaited=()):
@@ -419,8 +414,10 @@
         held = later
     wide = widen(rows, cols, scalars, at, blocks)
     acc = product(rows, cols, sources[: nrow - 1], panel, wide)
-    own = after(held, [acc])
-    sib = [to_sibling(x) for x in own]
+    (even,) = after(held[:1], [acc])
+    sib_even = to_sibling(even)
+    (odd,) = after(held[1:], [acc, sib_even])
+    own, sib = [even, odd], [sib_even, to_sibling(odd)]
     energies = (eps_virt, occ_rows, col_energy)
     return last(rows, cols, scalars, at, sources[nrow - 1 :], panel, own, sib, acc, energies)
 

time: 216 us -> 342 us (1.58)
  waiting for transfers between devices: 52.8 us -> 146 us
  Pallas kernels: 97.1 us -> 128 us
  blocking collectives: 23.6 us -> 0 us
  loops' own time: 1.04 us -> 16.9 us
  starting transfers between devices: 15.1 us -> 21.6 us
    ppermute x6, waiting for transfers between devices: 52.8 us -> 125 us  [around(): return lax.ppermute(x, 'row', ring)]
    all_to_all x1 -> x0, blocking collectives: 23.6 us -> none  [exchange(): return lax.all_to_all(x, 'col', split_axis=0, concat_axis=0, tiled=True)]
    all_to_all x1 -> x2, waiting for transfers between devices: 0.01 us -> 21.6 us  [exchange(): return lax.all_to_all(x, 'col', split_axis=0, concat_axis=0, tiled=True)]
    another operation x1, loops' own time: 1.04 us -> 16.9 us  [live_device(): lax.switch(index, [functools.partial(branch, size, nrow, ncol) for size i...]
    pallas_call x1, Pallas kernels: 18.2 us -> 29.4 us  [product(): pl.pallas_call(product_kernel, out_shape=jax.ShapeDtypeStruct((2, rows, B...]
    pallas_call x1, Pallas kernels: 18.5 us -> 25.2 us  [compact_ints(): pl.pallas_call(functools.partial(ints_kernel, rows, cols), out_shape=jax....]
    pallas_call x1, Pallas kernels: 18 us -> 23.9 us  [last(): pl.pallas_call(functools.partial(last_kernel, rows, cols), out_shape=jax....]
    all_to_all x1 -> x2, starting transfers between devices: 3.57 us -> 9.49 us  [exchange(): return lax.all_to_all(x, 'col', split_axis=0, concat_axis=0, tiled=True)]
  transfers between devices with their start and end apart: 17 -> 18, of which waited for: 4 -> 6; matrix products, arithmetic and copies ran while one was open for 2% -> 2% of each run, Pallas kernels for 36% -> 25%
where the time goes in v2:
time: 342 us; the launch traced here: 341 us
  waiting for transfers between devices  146 us (43%)
  Pallas kernels  128 us (37%)
  starting transfers between devices  21.6 us (6%)
  loops' own time  16.9 us (5%)
  between operations  14.9 us (4%)
  local copies, waits for them, and re-layouts  13.2 us (4%)
    ppermute x6, waiting for transfers between devices, around(): return lax.ppermute(x, 'row', ring)  125 us
    pallas_call x1, Pallas kernels, product(): pl.pallas_call(product_kernel, out_shape=jax.ShapeDtypeStruct((2, rows, B...  29.4 us
    pallas_call x1, Pallas kernels, compact_ints(): pl.pallas_call(functools.partial(ints_kernel, rows, cols), out_shape=jax....  25.2 us
    pallas_call x1, Pallas kernels, last(): pl.pallas_call(functools.partial(last_kernel, rows, cols), out_shape=jax....  23.9 us
    all_to_all x2, waiting for transfers between devices, exchange(): return lax.all_to_all(x, 'col', split_axis=0, concat_axis=0, tiled=True)  21.6 us
    pallas_call x1, Pallas kernels, widen(): pl.pallas_call(functools.partial(widen_kernel, rows, cols, slots), out_sh...  18.6 us
    another operation x1, loops' own time, live_device(): lax.switch(index, [functools.partial(branch, size, nrow, ncol) for size i...  16.9 us
    pallas_call x1, Pallas kernels, prep(): pl.pallas_call(functools.partial(prep_kernel, size), out_shape=(shape, sh...  15.9 us
  transfers between devices with their start and end apart: 18, of which 6 were waited for; matrix products, arithmetic and copies ran while one was open for 2% of the time, Pallas kernels for 25%

profile of v2, /device:TPU:0, one launch (start us, length us, event | category | flops | bytes accessed | tf_op | source)
XLA Modules:
  0.0 341.4 jit_solution(10518269112895676192)
XLA Ops:
  7.3 1.2 choose.1
  9.1 325.2 %conditional.1 = (f32[2048,1024]{1,0:T(8,128)}) conditional(s32[]{:T(128)} %bitcast.36, ((), s32[8]{0:T(128)}, s32[8]{0:T(128)}, s32[1]{0:T(128)}, bf16[2,8,16,16,8,64]{5,4,3,2,1,0:T(8,128)(2,1)}, /*index=5*/s32[2]{0:T(128)S(1)}, bf16[2048,1024]{1,0:T(8,128)(2,1)}, s32[]{:T(128)}, f32[8,64]{1,0:T(8,128)}, ...), branch_computations={%region_0.1_spmd, %region_1.2_spmd, %region_2.3_spmd, %region_3.4_... | conditional | flops 115964116992 | bytes 423672544 | solution.py:458
  17.3 15.9 %prep_amplitudes.5 = (bf16[8,128,896]{2,1,0:T(8,128)(2,1)}, bf16[8,128,896]{2,1,0:T(8,128)(2,1)}) custom-call(s32[8]{0:T(128)} %get-tuple-element.117.occ, s32[8]{0:T(128)} %get-tuple-element.118.virt, s32[1]{0:T(128)} %get-tuple-element.119.win, bf16[2,8,16,16,8,64]{5,4,3,2,1,0:T(8,128)(2,1)} %get-tuple-element.212.t2_ref), custom_call_target="tpu_custom_call" | custom-call | flops 7516192768 | bytes 12582912 | tf_op jit(solution)/shard_map/cond/branch_1_fun/prep_amplitudes/pallas_call | solution.py:92
  33.2 5.2 %all-to-all-start.2 = ((bf16[8,128,896]{2,1,0:T(8,128)(2,1)}), bf16[8,128,896]{2,1,0:T(8,128)(2,1)}, u32[]{:S(2)}, u32[]{:S(2)}) async-start(bf16[8,128,896]{2,1,0:T(8,128)(2,1)} %get-tuple-element.123), calls=%async_computation.2 | async-start | bytes 3670016 | tf_op jit(solution)/shard_map/cond/branch_1_fun/all_to_all | solution.py:397
  38.4 1.8 constant_dynamic-slice_fusion.9
  40.8 21.6 %all-to-all-done.2.x_ref = bf16[8,128,896]{2,1,0:T(8,128)(2,1)} async-done(((bf16[8,128,896]{2,1,0:T(8,128)(2,1)}), bf16[8,128,896]{2,1,0:T(8,128)(2,1)}, u32[]{:S(2)}, u32[]{:S(2)}) %all-to-all-start.2) | async-done | bytes 1835040 | tf_op jit(solution)/shard_map/cond/branch_1_fun/all_to_all | solution.py:397
  62.4 6.8 %compact_rows.10 = (bf16[896,896]{1,0:T(8,128)(2,1)}, bf16[8,128,896]{2,1,0:T(8,128)(2,1)}) custom-call(s32[8]{0:T(128)S(1)} %copy-done.26, s32[8]{0:T(128)S(1)} %copy-done.30, s32[1]{0:T(128)} %get-tuple-element.119.win, s32[2]{0:T(128)S(1)} %get-tuple-element.120.at, bf16[8,128,896]{2,1,0:T(8,128)(2,1)} %all-to-all-done.2.x_ref, ...), custom_call_target="tpu_custom_call", output_to_operand_aliasing={{1}: (5, {})} | custom-call | flops 3288334336 | bytes 3670016 | tf_op jit(solution)/shard_map/cond/branch_1_fun/compact_rows/pallas_call | solution.py:134
  69.1 4.3 %all-to-all-start.3 = ((bf16[8,128,896]{2,1,0:T(8,128)(2,1)}), bf16[8,128,896]{2,1,0:T(8,128)(2,1)}, u32[]{:S(2)}, u32[]{:S(2)}) async-start(bf16[8,128,896]{2,1,0:T(8,128)(2,1)} %get-tuple-element.125), calls=%async_computation.3 | async-start | bytes 3670016 | tf_op jit(solution)/shard_map/cond/branch_1_fun/all_to_all | solution.py:397
  73.5 2.1 collective-permute-start.16
  75.6 25.2 %compact_ints.5.refs_0_ = bf16[896,1792]{1,0:T(8,128)(2,1)} custom-call(s32[8]{0:T(128)S(1)} %copy-done.26, s32[8]{0:T(128)S(1)} %copy-done.30, s32[1]{0:T(128)} %get-tuple-element.119.win, s32[2]{0:T(128)S(1)} %get-tuple-element.120.at, bf16[2,32,2,16,1024]{4,3,2,1,0:T(8,128)(2,1)} %bitcast.68, bf16[1024,1024]{1,0:T(8,128)(2,1)} %collective-permute-done.15.other_ref, ...), custom_call_target="tpu_custom_call" | custom-call | flops 15032385536 | bytes 7405568 | tf_op jit(solution)/shard_map/cond/branch_1_fun/compact_ints/pallas_call | solution.py:189
  100.8 6.8 %compact_rows.11 = (bf16[896,896]{1,0:T(8,128)(2,1)}, bf16[896,1792]{1,0:T(8,128)(2,1)}) custom-call(s32[8]{0:T(128)S(1)} %copy-done.26, s32[8]{0:T(128)S(1)} %copy-done.30, s32[1]{0:T(128)} %get-tuple-element.119.win, s32[2]{0:T(128)S(1)} %get-tuple-element.120.at, bf16[8,128,896]{2,1,0:T(8,128)(2,1)} %all-to-all-done.3.x_ref, ...), custom_call_target="tpu_custom_call", output_to_operand_aliasing={{1}: (5, {})} | custom-call | flops 3288334336 | bytes 3670016 | tf_op jit(solution)/shard_map/cond/branch_1_fun/compact_rows/pallas_call | solution.py:134
  107.6 4.9 %collective-permute-done.16.refs_2_.refs_4_ = bf16[896,896]{1,0:T(8,128)(2,1)} collective-permute-done((bf16[896,896]{1,0:T(8,128)(2,1)}, bf16[896,896]{1,0:T(8,128)(2,1)}, u32[]{:S(2)}, u32[]{:S(2)}) %collective-permute-start.16) | collective-permute-done | bytes 1605664 | tf_op jit(solution)/shard_map/cond/branch_1_fun/ppermute | solution.py:394
  112.5 1.4 copy-done.12
  113.9 0.8 collective-permute-start.21
  114.8 3.4 collective-permute-start.17
  118.1 34.8 %collective-permute-done.21.refs_5_ = bf16[896,896]{1,0:T(8,128)(2,1)} collective-permute-done((bf16[896,896]{1,0:T(8,128)(2,1)S(1)}, bf16[896,896]{1,0:T(8,128)(2,1)}, u32[]{:S(2)}, u32[]{:S(2)}) %collective-permute-start.21) | collective-permute-done | bytes 1605664 | tf_op jit(solution)/shard_map/cond/branch_1_fun/ppermute | solution.py:394
  152.9 0.8 collective-permute-start.24
  154.2 1.1 copy-done.35
  155.3 32.0 %collective-permute-done.17.refs_8_ = bf16[896,896]{1,0:T(8,128)(2,1)} collective-permute-done((bf16[896,896]{1,0:T(8,128)(2,1)}, bf16[896,896]{1,0:T(8,128)(2,1)}, u32[]{:S(2)}, u32[]{:S(2)}) %collective-permute-start.17) | collective-permute-done | bytes 1605664 | tf_op jit(solution)/shard_map/cond/branch_1_fun/ppermute | solution.py:394
  187.3 33.2 %collective-permute-done.24.refs_9_ = bf16[896,896]{1,0:T(8,128)(2,1)} collective-permute-done((bf16[896,896]{1,0:T(8,128)(2,1)}, bf16[896,896]{1,0:T(8,128)(2,1)}, u32[]{:S(2)}, u32[]{:S(2)}) %collective-permute-start.24) | collective-permute-done | bytes 1605664 | tf_op jit(solution)/shard_map/cond/branch_1_fun/ppermute | solution.py:394
  222.3 3.4 collective-permute-start.27
  225.7 18.6 %widen.5.wide_ref = bf16[3,1792,1024]{2,1,0:T(8,128)(2,1)} custom-call(s32[8]{0:T(128)S(1)} %copy-done.26, s32[8]{0:T(128)S(1)} %copy-done.30, s32[1]{0:T(128)} %get-tuple-element.119.win, s32[2]{0:T(128)S(1)} %get-tuple-element.120.at, bf16[896,896]{1,0:T(8,128)(2,1)} %get-tuple-element.128.awaited.refs_0_, bf16[896,896]{1,0:T(8,128)(2,1)} %get-tuple-element.132.refs_1_, ...), custom_call_target="tpu_custom_call" | custom-call | flops 11274289152 | bytes 30277632 | tf_op jit(solution)/shard_map/cond/branch_1_fun/widen/pallas_call | solution.py:243
  244.3 29.4 %product.5.refs_1_.old_ref = f32[2,896,1024]{2,1,0:T(8,128)} custom-call(s32[3]{0:T(128)} %slice_bitcast_fusion.1.inner, bf16[4,2,896,1792]{3,2,1,0:T(8,128)(2,1)} %bitcast.80, bf16[3,1792,1024]{2,1,0:T(8,128)(2,1)} %widen.5.wide_ref), custom_call_target="tpu_custom_call" | custom-call | flops 39460012032 | bytes 20643840 | tf_op jit(solution)/shard_map/cond/branch_1_fun/product/pallas_call | solution.py:272
  273.7 1.2 copy-done.11
  274.9 19.9 %collective-permute-done.27.refs_0_ = bf16[896,896]{1,0:T(8,128)(2,1)S(1)} collective-permute-done((bf16[896,896]{1,0:T(8,128)(2,1)}, bf16[896,896]{1,0:T(8,128)(2,1)S(1)}, u32[]{:S(2)}, u32[]{:S(2)}) %collective-permute-start.27) | collective-permute-done | bytes 1605664 | tf_op jit(solution)/shard_map/cond/branch_1_fun/ppermute | solution.py:394
  294.8 1.2 copy-done.14
  296.0 1.2 copy-done.13
  298.5 0.7 fusion.4
  299.3 0.7 fusion.3
  300.0 0.7 copy.54.eocc_ref
  301.3 1.2 copy-done.36
  302.5 23.9 %last_product.5 = f32[2048,1024]{1,0:T(8,128)} custom-call(s32[8]{0:T(128)S(1)} %copy-done.26, s32[8]{0:T(128)S(1)} %copy-done.30, s32[1]{0:T(128)} %get-tuple-element.119.win, s32[2]{0:T(128)S(1)} %get-tuple-element.120.at, s32[1]{0:T(128)} %bitcast.9.inner, bf16[4,2,896,1792]{3,2,1,0:T(8,128)(2,1)} %bitcast.81, bf16[896,896]{1,0:T(8,128)(2,1)} %after.16.t0, ...), custom_call_target="tpu_custom_call" | custom-call | flops 13153337344 | bytes 21102592 | tf_op jit(solution)/shard_map/cond/branch_1_fun/last_product/pallas_call | solution.py:337
  (51 shorter events, 4.4 us)
Async XLA Ops:
  33.2 29.1 %all-to-all-start.2 = ((bf16[8,128,896]{2,1,0:T(8,128)(2,1)}), bf16[8,128,896]{2,1,0:T(8,128)(2,1)}, u32[]{:S(2)}, u32[]{:S(2)}) async-start(bf16[8,128,896]{2,1,0:T(8,128)(2,1)} %get-tuple-element.123), calls=%async_computation.2 | async-start | bytes 3670016 | tf_op jit(solution)/shard_map/cond/branch_1_fun/all_to_all | solution.py:397
  38.4 23.9 %copy-start.26 = (s32[8]{0:T(128)S(1)}, s32[8]{0:T(128)}, u32[]{:S(2)}) copy-start(s32[8]{0:T(128)} %get-tuple-element.117.occ) | copy-start | bytes 100 | tf_op jit(solution)/shard_map/cond
  38.4 23.9 %copy-start.30 = (s32[8]{0:T(128)S(1)}, s32[8]{0:T(128)}, u32[]{:S(2)}) copy-start(s32[8]{0:T(128)} %get-tuple-element.118.virt) | copy-start | bytes 100 | tf_op jit(solution)/shard_map/cond
  40.2 35.4 %collective-permute-start.15 = (bf16[1024,1024]{1,0:T(8,128)(2,1)S(1)}, bf16[1024,1024]{1,0:T(8,128)(2,1)}, u32[]{:S(2)}, u32[]{:S(2)}) collective-permute-start(bf16[1024,1024]{1,0:T(8,128)(2,1)S(1)} %bitcast.75), channel_id=1, source_target_pairs={{0,1},{1,0},{2,3},{3,2},{4,5},{5,4},{6,7},{7,6},{8,9},{9,8},{10,11... | collective-permute-start | bytes 6291464 | tf_op jit(solution)/shard_map/cond/branch_1_fun/ppermute | solution.py:391
  69.1 31.7 %all-to-all-start.3 = ((bf16[8,128,896]{2,1,0:T(8,128)(2,1)}), bf16[8,128,896]{2,1,0:T(8,128)(2,1)}, u32[]{:S(2)}, u32[]{:S(2)}) async-start(bf16[8,128,896]{2,1,0:T(8,128)(2,1)} %get-tuple-element.125), calls=%async_computation.3 | async-start | bytes 3670016 | tf_op jit(solution)/shard_map/cond/branch_1_fun/all_to_all | solution.py:397
  73.4 170.8 %all-gather.11.cloned.1.call-start = ((), (), s32[]{:S(2)}) async-start(), calls=%async_computation.9 | async-start | bytes 28901376 | tf_op jit(solution)/shard_map/cond/branch_1_fun/all_gather | solution.py:407
  73.5 39.0 %collective-permute-start.16 = (bf16[896,896]{1,0:T(8,128)(2,1)}, bf16[896,896]{1,0:T(8,128)(2,1)}, u32[]{:S(2)}, u32[]{:S(2)}) collective-permute-start(bf16[896,896]{1,0:T(8,128)(2,1)} %get-tuple-element.128.awaited.refs_0_), channel_id=1, source_target_pairs={{0,8},{8,24},{24,16},{16,0},{1,9},{9,25},{25,17},{17,1},{2,10},{10... | collective-permute-start | bytes 4816904 | tf_op jit(solution)/shard_map/cond/branch_1_fun/ppermute | solution.py:394
  112.5 1.4 copy-start.12
  112.5 2.2 copy-start.34
  113.9 39.0 %collective-permute-start.21 = (bf16[896,896]{1,0:T(8,128)(2,1)S(1)}, bf16[896,896]{1,0:T(8,128)(2,1)}, u32[]{:S(2)}, u32[]{:S(2)}) collective-permute-start(bf16[896,896]{1,0:T(8,128)(2,1)S(1)} %copy-done.12), channel_id=1, source_target_pairs={{0,8},{8,24},{24,16},{16,0},{1,9},{9,25},{25,17},{17,1},{2,10},{10... | collective-permute-start | bytes 4816904 | tf_op jit(solution)/shard_map/cond/branch_1_fun/ppermute | solution.py:394
  114.8 39.4 %collective-permute-start.19 = (bf16[896,896]{1,0:T(8,128)(2,1)S(1)}, bf16[896,896]{1,0:T(8,128)(2,1)S(1)}, u32[]{:S(2)}, u32[]{:S(2)}) collective-permute-start(bf16[896,896]{1,0:T(8,128)(2,1)S(1)} %copy-done.34), channel_id=1, source_target_pairs={{0,1},{1,0},{2,3},{3,2},{4,5},{5,4},{6,7},{7,6},{8,9},{9,8},{10,11... | collective-permute-start | bytes 4816904 | tf_op jit(solution)/shard_map/cond/branch_1_fun/ppermute | solution.py:391
  114.8 72.6 %collective-permute-start.17 = (bf16[896,896]{1,0:T(8,128)(2,1)}, bf16[896,896]{1,0:T(8,128)(2,1)}, u32[]{:S(2)}, u32[]{:S(2)}) collective-permute-start(bf16[896,896]{1,0:T(8,128)(2,1)} %collective-permute-done.16.refs_2_.refs_4_), channel_id=1, source_target_pairs={{0,8},{8,24},{24,16},{16,0},{1,9},{9,25},{25,17},{17,1},{2,10},{10... | collective-permute-start | bytes 4816904 | tf_op jit(solution)/shard_map/cond/branch_1_fun/ppermute | solution.py:394
  152.9 67.6 %collective-permute-start.24 = (bf16[896,896]{1,0:T(8,128)(2,1)}, bf16[896,896]{1,0:T(8,128)(2,1)}, u32[]{:S(2)}, u32[]{:S(2)}) collective-permute-start(bf16[896,896]{1,0:T(8,128)(2,1)} %collective-permute-done.21.refs_5_), channel_id=1, source_target_pairs={{0,8},{8,24},{24,16},{16,0},{1,9},{9,25},{25,17},{17,1},{2,10},{10... | collective-permute-start | bytes 4816904 | tf_op jit(solution)/shard_map/cond/branch_1_fun/ppermute | solution.py:394
  153.7 68.1 %collective-permute-start.20 = (bf16[896,896]{1,0:T(8,128)(2,1)S(1)}, bf16[896,896]{1,0:T(8,128)(2,1)}, u32[]{:S(2)}, u32[]{:S(2)}) collective-permute-start(bf16[896,896]{1,0:T(8,128)(2,1)S(1)} %copy-done.12), channel_id=1, source_target_pairs={{0,1},{1,0},{2,3},{3,2},{4,5},{5,4},{6,7},{7,6},{8,9},{9,8},{10,11... | collective-permute-start | bytes 4816904 | tf_op jit(solution)/shard_map/cond/branch_1_fun/ppermute | solution.py:391
  153.7 68.6 %collective-permute-start.22 = (bf16[896,896]{1,0:T(8,128)(2,1)}, bf16[896,896]{1,0:T(8,128)(2,1)}, u32[]{:S(2)}, u32[]{:S(2)}) collective-permute-start(bf16[896,896]{1,0:T(8,128)(2,1)} %collective-permute-done.16.refs_2_.refs_4_), channel_id=1, source_target_pairs={{0,1},{1,0},{2,3},{3,2},{4,5},{5,4},{6,7},{7,6},{8,9},{9,8},{10,11... | collective-permute-start | bytes 4816904 | tf_op jit(solution)/shard_map/cond/branch_1_fun/ppermute | solution.py:391
  154.2 1.1 copy-start.35
  155.3 70.3 %collective-permute-start.23 = (bf16[896,896]{1,0:T(8,128)(2,1)}, bf16[896,896]{1,0:T(8,128)(2,1)}, u32[]{:S(2)}, u32[]{:S(2)}) collective-permute-start(bf16[896,896]{1,0:T(8,128)(2,1)} %collective-permute-done.21.refs_5_), channel_id=1, source_target_pairs={{0,1},{1,0},{2,3},{3,2},{4,5},{5,4},{6,7},{7,6},{8,9},{9,8},{10,11... | collective-permute-start | bytes 4816904 | tf_op jit(solution)/shard_map/cond/branch_1_fun/ppermute | solution.py:391
  187.3 38.3 %collective-permute-start.25 = (bf16[896,896]{1,0:T(8,128)(2,1)}, bf16[896,896]{1,0:T(8,128)(2,1)}, u32[]{:S(2)}, u32[]{:S(2)}) collective-permute-start(bf16[896,896]{1,0:T(8,128)(2,1)} %collective-permute-done.17.refs_8_), channel_id=1, source_target_pairs={{0,1},{1,0},{2,3},{3,2},{4,5},{5,4},{6,7},{7,6},{8,9},{9,8},{10,11... | collective-permute-start | bytes 4816904 | tf_op jit(solution)/shard_map/cond/branch_1_fun/ppermute | solution.py:391
  220.5 5.1 %collective-permute-start.26 = (bf16[896,896]{1,0:T(8,128)(2,1)}, bf16[896,896]{1,0:T(8,128)(2,1)}, u32[]{:S(2)}, u32[]{:S(2)}) collective-permute-start(bf16[896,896]{1,0:T(8,128)(2,1)} %collective-permute-done.24.refs_9_), channel_id=1, source_target_pairs={{0,1},{1,0},{2,3},{3,2},{4,5},{5,4},{6,7},{7,6},{8,9},{9,8},{10,11... | collective-permute-start | bytes 4816904 | tf_op jit(solution)/shard_map/cond/branch_1_fun/ppermute | solution.py:391
  221.8 51.9 %collective-permute-start.18 = (bf16[896,896]{1,0:T(8,128)(2,1)}, bf16[896,896]{1,0:T(8,128)(2,1)S(1)}, u32[]{:S(2)}, u32[]{:S(2)}) collective-permute-start(bf16[896,896]{1,0:T(8,128)(2,1)} %collective-permute-done.17.refs_8_), channel_id=1, source_target_pairs={{0,8},{8,24},{24,16},{16,0},{1,9},{9,25},{25,17},{17,1},{2,10},{10... | collective-permute-start | bytes 4816904 | tf_op jit(solution)/shard_map/cond/branch_1_fun/ppermute | solution.py:394
  222.3 72.5 %collective-permute-start.27 = (bf16[896,896]{1,0:T(8,128)(2,1)}, bf16[896,896]{1,0:T(8,128)(2,1)S(1)}, u32[]{:S(2)}, u32[]{:S(2)}) collective-permute-start(bf16[896,896]{1,0:T(8,128)(2,1)} %collective-permute-done.24.refs_9_), channel_id=1, source_target_pairs={{0,8},{8,24},{24,16},{16,0},{1,9},{9,25},{25,17},{17,1},{2,10},{10... | collective-permute-start | bytes 4816904 | tf_op jit(solution)/shard_map/cond/branch_1_fun/ppermute | solution.py:394
  273.7 1.2 copy-start.11
  274.9 23.5 %copy-start.22 = (f32[8,64]{1,0:T(8,128)S(1)}, f32[8,64]{1,0:T(8,128)}, u32[]{:S(2)}) copy-start(f32[8,64]{1,0:T(8,128)} %get-tuple-element.334) | copy-start | bytes 6148 | tf_op jit(solution)/shard_map/cond
  274.9 19.9 %collective-permute-start.28 = (bf16[896,896]{1,0:T(8,128)(2,1)}, bf16[896,896]{1,0:T(8,128)(2,1)S(1)}, u32[]{:S(2)}, u32[]{:S(2)}) collective-permute-start(bf16[896,896]{1,0:T(8,128)(2,1)} %after.16.t0), channel_id=1, source_target_pairs={{0,1},{1,0},{2,3},{3,2},{4,5},{5,4},{6,7},{7,6},{8,9},{9,8},{10,11... | collective-permute-start | bytes 4816904 | tf_op jit(solution)/shard_map/cond/branch_1_fun/ppermute | solution.py:391
  294.8 1.2 copy-start.14
  296.0 1.2 copy-start.13
  297.1 4.2 %collective-permute-start.29 = (bf16[896,896]{1,0:T(8,128)(2,1)}, bf16[896,896]{1,0:T(8,128)(2,1)S(1)}, u32[]{:S(2)}, u32[]{:S(2)}) collective-permute-start(bf16[896,896]{1,0:T(8,128)(2,1)} %after.17.t1), channel_id=1, source_target_pairs={{0,1},{1,0},{2,3},{3,2},{4,5},{5,4},{6,7},{7,6},{8,9},{9,8},{10,11... | collective-permute-start | bytes 4816904 | tf_op jit(solution)/shard_map/cond/branch_1_fun/ppermute | solution.py:391
  301.3 1.2 copy-start.36
Sparse Core Ops, SparseCore 0:
  112.7 128.9 all-gather.10
